TPU v7x, 512 devices: a whole 4x8x8 slice. The times are simulated.
512 devices in a mesh: ha: 16 (over y_lo, z), wa: 16 (over y_hi, x), ta: 2 (over core).
Axes of the slice: x: 4, y: 8 (y_hi: 4, y_lo: 2; y = y_hi * 2 + y_lo), z: 8, core: 2. Of those that a mesh axis runs over, the one named last changes fastest.
Arguments:
- queries: bfloat16 [128, 256, 1536], P('ha', 'wa', 'ta'), may hold values from -6 to 6
- keys_values: bfloat16 [2, 128, 256, 1536], P(None, 'ha', 'wa', 'ta'), may hold values from -6 to 6
- grad_out: bfloat16 [128, 256, 1536], P('ha', 'wa', 'ta'), may hold values from -96 to 96
- log_totals: float32 [128, 256, 12], P('ha', 'wa', 'ta'), may hold values from 6 to 8
- row_deltas: float32 [128, 256, 12], P('ha', 'wa', 'ta'), may hold values from -256 to 256
- prompt_kv: bfloat16 [2, 128, 1536], P(None, None, 'ta'), may hold values from -6 to 6
- prompt_proj: bfloat16 [2, 3072, 1536], P(None, 'ha', 'ta'), may hold values from -0.109375 to 0.109375
- neighbours: int32 [512, 9], replicated, may hold values from -1 to 511, as said below
- prompt_length: int32 [1], replicated, may hold values from 32 to 128
Outputs:
- grad_queries: bfloat16 [128, 256, 1536], P('ha', 'wa', 'ta')
- grad_keys_values: bfloat16 [2, 128, 256, 1536], P(None, 'ha', 'wa', 'ta')
- context_grad: float32 [128, 3072], P(None, 'ha')
Inputs may be any that keep to these rules, and one draw needn't show every extreme that they name: `neighbours`: row t lists tile t first, then further tiles, without repeats, each within one tile of tile t in both directions, then -1 in the unused slots.
All inputs are finite; a program needn't handle non-finite values.
Results may differ from a plain program's by a relative error of at most 0.005.
Values may be sent and summed in bfloat16 or wider, within the bound.
A program may use at most 64 MiB of HBM per device.

v0:
```python
import jax
import jax.numpy as jnp
from jax import lax
from jax.sharding import PartitionSpec as P

TS = 8


NEIGHBOUR_STEPS = [(row_step, col_step) for row_step in (-1, 0, 1) for col_step in (-1, 0, 1)]


def shifted_2(x, axis, by):
    length = lax.axis_size(axis)
    pairs = [(i, i + by) for i in range(length) if 0 <= i + by < length]
    return lax.ppermute(x, axis, pairs)


def padded(cells, sides, width):
    for axis, dim in sides:
        count = lax.axis_size(axis)
        ends = count - 1
        head = lax.slice_in_dim(cells, 0, width, axis=dim)
        tail = lax.slice_in_dim(cells, cells.shape[dim] - width, cells.shape[dim], axis=dim)
        cells = jnp.concatenate(
            [
                lax.ppermute(tail, axis, [(i, (i + 1) % count) for i in range(ends)]),
                cells,
                lax.ppermute(head, axis, [((i + 1) % count, i) for i in range(ends)]),
            ],
            axis=dim,
        )
    return cells


def tile_grid(values_field, tile_side):
    height, breadth = (values_field.shape[0], values_field.shape[1])
    remains = values_field.shape[2:]
    blocks = values_field.reshape(
        (height // tile_side, tile_side, breadth // tile_side, tile_side) + remains
    )
    blocks = jnp.swapaxes(blocks, 1, 2)
    return blocks.reshape(
        (height // tile_side, breadth // tile_side, tile_side * tile_side) + remains
    )


def untile(tile_field, tile_side):
    remains = tile_field.shape[3:]
    blocks = tile_field.reshape(tile_field.shape[:2] + (tile_side, tile_side) + remains)
    blocks = jnp.swapaxes(blocks, 1, 2)
    return blocks.reshape(
        (tile_field.shape[0] * tile_side, tile_field.shape[1] * tile_side) + remains
    )


def block_grads(queries, out_grads, log_total, row_delta, key_rows, value_rows, allowed):
    factor = queries.shape[-1] ** (-0.5)
    scores = (
        jnp.einsum("nmhe,nkhe->nhmk", queries, key_rows, preferred_element_type=jnp.float32)
        * factor
    )
    shifted = scores - jnp.swapaxes(log_total, 1, 2)[..., None]
    probability = jnp.where(allowed[:, None, None, :], jnp.exp(shifted), 0.0)
    prob_grads = jnp.einsum(
        "nmhe,nkhe->nhmk", out_grads, value_rows, preferred_element_type=jnp.float32
    )
    score_grads = (
        factor * probability * (prob_grads - jnp.swapaxes(row_delta, 1, 2)[..., None])
    ).astype(jnp.bfloat16)
    grad_q = jnp.einsum(
        "nhmk,nkhe->nmhe", score_grads, key_rows, preferred_element_type=jnp.float32
    )
    grad_k = jnp.einsum("nhmk,nmhe->nkhe", score_grads, queries, preferred_element_type=jnp.float32)
    grad_v = jnp.einsum(
        "nhmk,nmhe->nkhe",
        probability.astype(jnp.bfloat16),
        out_grads,
        preferred_element_type=jnp.float32,
    )
    return (grad_q, grad_k, grad_v)


def region_allowed(neighbours, grid_rows, grid_cols, first_row, first_col, span_rows, span_cols):
    slot_count = neighbours.shape[-1]
    listed = jnp.pad(
        neighbours.reshape(grid_rows, grid_cols, slot_count),
        ((1, 1), (1, 1), (0, 0)),
        constant_values=-1,
    )
    listed = lax.dynamic_slice(
        listed, (first_row, first_col, 0), (span_rows, span_cols, slot_count)
    )
    tile_row = first_row - 2 + lax.broadcasted_iota(jnp.int32, (span_rows + 2, span_cols + 2), 0)
    tile_col = first_col - 2 + lax.broadcasted_iota(jnp.int32, (span_rows + 2, span_cols + 2), 1)
    inside = (tile_row >= 0) & (tile_row < grid_rows) & (tile_col >= 0) & (tile_col < grid_cols)
    numbers = jnp.where(inside, tile_row * grid_cols + tile_col, -2)
    mask_list = []
    for row_step, col_step in NEIGHBOUR_STEPS:
        target = numbers[
            1 + row_step : 1 + row_step + span_rows, 1 + col_step : 1 + col_step + span_cols
        ]
        mask_list.append(jnp.any(listed == target[:, :, None], axis=-1))
    return jnp.stack(mask_list, axis=-1)


def tile_mask(plane, cells):
    return jnp.broadcast_to(plane.reshape(-1, 1), (plane.size, cells))


def fold_rims(spread, rows_here, cols_here):
    west_strip = spread[:, :, :TS]
    east_strip = spread[:, :, TS + cols_here :]
    from_east = shifted_2(west_strip, "wa", -1)
    from_west = shifted_2(east_strip, "wa", 1)
    middle = spread[:, :, TS : TS + cols_here]
    middle = middle.at[:, :, :TS].add(from_west)
    middle = middle.at[:, :, cols_here - TS :].add(from_east)
    north_strip = middle[:, :TS]
    south_strip = middle[:, TS + rows_here :]
    from_south = shifted_2(north_strip, "ha", -1)
    from_north = shifted_2(south_strip, "ha", 1)
    inner = middle[:, TS : TS + rows_here]
    inner = inner.at[:, :TS].add(from_north)
    inner = inner.at[:, rows_here - TS :].add(from_south)
    return inner


def local(
    queries,
    keys_values,
    grad_out,
    log_totals,
    row_deltas,
    prompt_kv,
    prompt_proj,
    neighbours,
    prompt_length,
):
    rows_here, cols_here, width = queries.shape
    head_count = log_totals.shape[-1]
    head_width = width // head_count
    cells = TS * TS
    own_rows, own_cols = (rows_here // TS, cols_here // TS)
    tile_count = own_rows * own_cols
    grid_rows = own_rows * lax.axis_size("ha")
    grid_cols = own_cols * lax.axis_size("wa")
    first_row = lax.axis_index("ha") * own_rows
    first_col = lax.axis_index("wa") * own_cols
    allowed = region_allowed(
        neighbours, grid_rows, grid_cols, first_row, first_col, own_rows + 2, own_cols + 2
    )

    def heads_tiles(values_field):
        return tile_grid(
            values_field.reshape(values_field.shape[:-1] + (head_count, head_width)), TS
        )

    def flatten(tile_field):
        return tile_field.reshape((tile_count,) + tile_field.shape[2:])

    own_q = flatten(heads_tiles(queries))
    own_g = flatten(heads_tiles(grad_out))
    own_t = flatten(tile_grid(log_totals, TS))
    own_d = flatten(tile_grid(row_deltas, TS))
    region = padded(keys_values, (("ha", 1), ("wa", 2)), TS)
    region_keys = heads_tiles(region[0])
    region_values = heads_tiles(region[1])
    grad_query = jnp.zeros(own_q.shape, jnp.float32)
    key_sums = jnp.zeros(region_keys.shape, jnp.float32)
    value_sums = jnp.zeros(region_values.shape, jnp.float32)
    for step_index, (row_step, col_step) in enumerate(NEIGHBOUR_STEPS):
        row_from, col_from = (1 + row_step, 1 + col_step)
        near_keys = flatten(
            region_keys[row_from : row_from + own_rows, col_from : col_from + own_cols]
        )
        near_values = flatten(
            region_values[row_from : row_from + own_rows, col_from : col_from + own_cols]
        )
        near_mask = tile_mask(allowed[1 : 1 + own_rows, 1 : 1 + own_cols, step_index], cells)
        parts = block_grads(own_q, own_g, own_t, own_d, near_keys, near_values, near_mask)
        grad_query = grad_query + parts[0]
        shaped = (own_rows, own_cols) + parts[1].shape[1:]
        key_sums = key_sums.at[row_from : row_from + own_rows, col_from : col_from + own_cols].add(
            parts[1].reshape(shaped)
        )
        value_sums = value_sums.at[
            row_from : row_from + own_rows, col_from : col_from + own_cols
        ].add(parts[2].reshape(shaped))
    spread = jnp.stack([untile(key_sums, TS), untile(value_sums, TS)])
    spread = spread.reshape(spread.shape[:3] + (width,))
    kv_grads = fold_rims(spread, rows_here, cols_here)
    prompt_rows = prompt_kv.shape[1]
    live = lax.broadcasted_iota(jnp.int32, (1, prompt_rows), 1) < prompt_length[0]
    prompt_keys = prompt_kv[0].reshape((1, prompt_rows, head_count, head_width))
    prompt_values = prompt_kv[1].reshape((1, prompt_rows, head_count, head_width))
    flat_rows = (1, tile_count * cells, head_count, head_width)
    prompt_parts = block_grads(
        own_q.reshape(flat_rows),
        own_g.reshape(flat_rows),
        own_t.reshape(1, tile_count * cells, head_count),
        own_d.reshape(1, tile_count * cells, head_count),
        prompt_keys,
        prompt_values,
        live,
    )
    grad_query = grad_query + prompt_parts[0].reshape(own_q.shape)
    partial_sums = jnp.stack([prompt_parts[1][0], prompt_parts[2][0]]).reshape(
        2, prompt_rows, width
    )
    prompt_total = lax.psum(partial_sums, ("ha", "wa")).astype(jnp.bfloat16)
    context_part = jnp.einsum(
        "tf,cf->tc", prompt_total[0], prompt_proj[0], preferred_element_type=jnp.float32
    )
    context_part = context_part + jnp.einsum(
        "tf,cf->tc", prompt_total[1], prompt_proj[1], preferred_element_type=jnp.float32
    )
    context_grad = lax.psum(context_part, "ta")
    grad_queries = untile(grad_query.reshape((own_rows, own_cols) + grad_query.shape[1:]), TS)
    grad_queries = grad_queries.reshape(rows_here, cols_here, width).astype(jnp.bfloat16)
    return (grad_queries, kv_grads.astype(jnp.bfloat16), context_grad)


def solution(mesh):
    placed = (
        P("ha", "wa", "ta"),
        P(None, "ha", "wa", "ta"),
        P("ha", "wa", "ta"),
        P("ha", "wa", "ta"),
        P("ha", "wa", "ta"),
        P(None, None, "ta"),
        P(None, "ha", "ta"),
        P(),
        P(),
    )
    return jax.shard_map(
        local,
        mesh=mesh,
        in_specs=placed,
        out_specs=(P("ha", "wa", "ta"), P(None, "ha", "wa", "ta"), P(None, "ha")),
        check_vma=False,
    )
```

profile of v0, /device:TPU:8, one launch (start us, length us, event | category | flops | bytes accessed | tf_op | source)
XLA Modules:
  0.0 1773.5 jit_solution(9273454220476609833)
XLA Ops:
  7.2 4.3 collective-permute-start
  11.5 8.5 collective-permute-start.1
  20.7 1.4 and_reduce_fusion
  22.2 0.8 reshape.1174
  23.2 0.8 reshape.1177
  24.7 0.8 reshape.1173
  25.6 0.6 slice_bitcast_fusion.57
  26.2 0.7 compare_reduce_fusion
  27.0 0.7 slice_bitcast_fusion.49
  28.2 0.6 slice_bitcast_fusion.55
  28.8 0.6 slice_bitcast_fusion.54
  30.0 0.6 slice_bitcast_fusion.52
  30.7 1.0 copy.146
  31.6 1.0 copy.143
  32.6 1.1 fusion.188
  35.0 1.0 pad_maximum_fusion.2
  36.2 3.4 collective-permute-start.2
  39.6 1.3 collective-permute-start.3
  40.9 0.6 fusion.190
  41.5 0.9 reshape_reshape.22
  42.4 0.9 reshape_reshape.25
  43.4 0.6 fusion.191
  43.9 0.8 slice_bitcast_fusion.51
  44.7 0.7 slice_bitcast_fusion.50
  45.4 6.5 collective-permute-done.2
  51.9 4.1 collective-permute-done.3
  62.8 1.5 fusion.44
  64.3 2.1 fusion.47
  68.3 1.5 fusion.61
  69.8 2.1 fusion.64
  73.5 1.2 fusion.77
  74.7 0.7 copy-done.1
  75.3 4.4 collective-permute-start.4
  79.7 1640.1 %all-reduce.7 = bf16[2,128,768]{1,2,0:T(8,128)(2,1)} all-reduce(f32[2,128,768]{1,2,0:T(8,128)} %bitcast.599), channel_id=1, replica_groups=mesh['ha'=16,'wa'=16,'ta'=2] {'ha','wa'}, use_global_device_ids=true, to_apply=%region_10.11 | all-reduce | flops 196608 | bytes 1179648 | tf_op jit(solution)/shard_map/psum | solution.py:210
  1719.8 1.2 fusion.97
  1721.0 1.9 convolution_add_fusion.8
  1722.9 1.3 fusion.192
  1724.2 1.7 fusion
  1726.2 1.6 pad_maximum_fusion.1
  1727.9 1.4 collective-permute-start.5
  1730.7 15.4 collective-permute-done.5
  1746.6 2.1 collective-permute-start.6
  1748.6 6.0 collective-permute-start.7
  1755.8 0.7 copy.328
  1756.5 6.2 collective-permute-done.6
  1762.7 1.5 collective-permute-done.7
  1764.2 0.9 fusion.95
  1765.1 1.5 copy.357
  (153 shorter events, 16.3 us)
Async XLA Ops:
  7.2 1757.9 %all-reduce.6.cloned.1.call-start = ((), (), s32[]{:S(2)}) async-start(), calls=%async_computation | async-start | bytes 196608 | tf_op jit(solution)/shard_map/psum | solution.py:217
  7.2 28.8 %collective-permute-start = (bf16[2,8,16,768]{3,2,1,0:T(8,128)(2,1)}, bf16[2,8,16,768]{3,2,1,0:T(8,128)(2,1)S(1)}, u32[]{:S(2)}, u32[]{:S(2)}) collective-permute-start(bf16[2,8,16,768]{3,2,1,0:T(8,128)(2,1)} %param.58), channel_id=1, source_target_pairs={{0,32},{32,64},{64,96},{96,128},{128,160},{160,192},{192,224},{224... | collective-permute-start | bytes 1179656 | tf_op jit(solution)/shard_map/ppermute | solution.py:26
  11.5 24.6 %collective-permute-start.1 = (bf16[2,8,16,768]{3,2,1,0:T(8,128)(2,1)}, bf16[2,8,16,768]{3,2,1,0:T(8,128)(2,1)S(1)}, u32[]{:S(2)}, u32[]{:S(2)}) collective-permute-start(bf16[2,8,16,768]{3,2,1,0:T(8,128)(2,1)} %param.58), channel_id=1, source_target_pairs={{32,0},{64,32},{96,64},{128,96},{160,128},{192,160},{224,192},{256... | collective-permute-start | bytes 1179656 | tf_op jit(solution)/shard_map/ppermute | solution.py:28
  23.1 1.1 copy-start.24
  24.0 0.6 copy-start.25
  33.8 2.1 copy-start.23
  34.2 1.8 copy-start.26
  34.5 1.6 copy-start.16
  36.2 15.7 collective-permute-start.2
  39.6 16.4 collective-permute-start.3
  56.5 0.9 copy-start.3
  56.5 0.9 copy-start.33
  56.5 1.2 copy-start.27
  56.9 1.1 copy-start
  58.4 3.9 copy-start.19
  58.4 1.3 copy-start.32
  58.7 8.8 copy-start.17
  58.9 1.3 copy-start.31
  59.2 8.1 copy-start.4
  59.4 1.3 copy-start.30
  59.7 7.4 copy-start.6
  60.0 1.3 copy-start.29
  60.2 6.6 copy-start.8
  60.5 1.3 copy-start.28
  60.7 5.9 copy-start.10
  61.2 5.2 copy-start.12
  61.8 2.5 copy-start.14
  62.3 2.0 copy-start.21
  73.5 1.9 copy-start.1
  75.3 1650.7 %collective-permute-start.4 = (f32[2,24,8,768]{3,2,1,0:T(8,128)}, f32[2,24,8,768]{3,2,1,0:T(8,128)}, u32[]{:S(2)}, u32[]{:S(2)}) collective-permute-start(f32[2,24,8,768]{3,2,1,0:T(8,128)} %fusion.77), channel_id=1, source_target_pairs={{0,2},{2,4},{4,6},{6,8},{8,10},{10,12},{12,14},{14,16},{16,18},{18... | collective-permute-start | bytes 3538952 | tf_op jit(solution)/shard_map/ppermute | solution.py:15
  1724.2 2.0 copy-start.2
  1726.0 3.3 copy-start.20
  1726.0 3.6 copy-start.22
  1726.0 3.9 copy-start.15
  1727.9 2.3 copy-start.13
  1727.9 2.5 copy-start.11
  1727.9 18.2 %collective-permute-start.5 = (f32[2,24,8,768]{3,2,1,0:T(8,128)S(1)}, f32[2,24,8,768]{3,2,1,0:T(8,128)S(1)}, u32[]{:S(2)}, u32[]{:S(2)}) collective-permute-start(f32[2,24,8,768]{3,2,1,0:T(8,128)S(1)} %get-tuple-element.291), channel_id=1, source_target_pairs={{2,0},{4,2},{6,4},{8,6},{10,8},{12,10},{14,12},{16,14},{18,16},{20... | collective-permute-start | bytes 3538952 | tf_op jit(solution)/shard_map/ppermute | solution.py:15
  1746.4 8.3 copy-start.9
  1746.4 8.5 copy-start.7
  1746.4 8.8 copy-start.5
  1746.6 8.9 copy-start.18
  1746.6 16.1 collective-permute-start.6
  1748.6 15.5 collective-permute-start.7
Sparse Core Ops, SparseCore 0:
  1723.1 23.5 all-reduce.5
where the time goes:
time: 1770 us
  blocking collectives  1640 us (93%)
  waiting for transfers between devices  33.8 us (2%)
  starting transfers between devices  31.4 us (2%)
  matrix products  22 us (1%)
  local copies, waits for them, and re-layouts  20.9 us (1%)
    psum x1, blocking collectives, local(): prompt_total = lax.psum(partial_sums, ('ha', 'wa')).astype(jnp.bfloat16)  1640 us
  transfers between devices with their start and end apart: 9, of which 5 were waited for; matrix products, arithmetic and copies ran while one was open for 2% of the time, Pallas kernels for 0%

commit v1 on v0

v1 whole, which is shorter than its diff:
```python
import functools

import jax
import jax.numpy as jnp
from jax import lax
from jax.experimental import pallas as pl
from jax.experimental.pallas import tpu as pltpu
from jax.sharding import PartitionSpec as P

MESH = pl.DeviceIdType.MESH
F32 = jnp.float32
BF16 = jnp.bfloat16
TS = 8
CELLS = TS * TS
HD = 128
BIG = 1e30
STEPS = [(-1, 0), (1, 0), (0, -1), (0, 1), (-1, -1), (-1, 1), (1, -1), (1, 1)]


def block_of(row_step, col_step):
    return row_step + 1 if col_step == 0 else row_step + 4


def rows_of(col_step):
    return {0: slice(0, 128), -1: slice(0, 64), 1: slice(64, 128)}[col_step]


def nt(a, b):
    return lax.dot_general(a, b, (((1,), (1,)), ((), ())), preferred_element_type=F32)


def nn(a, b):
    return lax.dot_general(a, b, (((1,), (0,)), ((), ())), preferred_element_type=F32)


def tn(a, b):
    return lax.dot_general(a, b, (((0,), (0,)), ((), ())), preferred_element_type=F32)


def kernel(
    nh, nw, heads, per_owner,
    q_hbm, kv_hbm, g_hbm, lt_hbm, rd_hbm, pkv_hbm, proj_hbm, nb_hbm, plen_ref,
    dq_out, dkv_out, ctx_out,
    qn, kv, gn, ltn, rdn, pkv, proj, nb,
    qg, lrx, lro, pen, picked, dq_acc, dq_send, dq_recv, dkv_acc,
    ps, pr, t2, r2, s2, g2, c3, c4,
    ld_sem, qg_ss, qg_rs, lr_ss, lr_rs, dq_ss, dq_rs,
    p1_ss, p1_rs, p2_ss, p2_rs, p3_ss, p3_rs, c3_ss, c3_rs, c4_ss, c4_rs,
):
    width = heads * HD
    ia, iw, it = lax.axis_index("ha"), lax.axis_index("wa"), lax.axis_index("ta")
    factor = HD ** -0.5
    tr = 128 // nw

    def at(row_step, col_step):
        return (lax.rem(ia + row_step + nh, nh), lax.rem(iw + col_step + nw, nw), it)

    barrier = pltpu.get_barrier_semaphore()

    def greet(who):
        pl.semaphore_signal(barrier, inc=1, device_id=who, device_id_type=MESH)

    def greet_wa(i, c):
        greet((ia, lax.rem(iw + i, nw), it))
        return c

    def greet_ha(i, c):
        greet((lax.rem(ia + i, nh), iw, it))
        return c

    for step in STEPS[4:]:
        greet(at(*step))
    lax.fori_loop(1, nw, greet_wa, 0)
    lax.fori_loop(1, nh, greet_ha, 0)
    greet((ia, iw, 1 - it))

    loads = [
        pltpu.make_async_copy(src, dst, ld_sem.at[n])
        for n, (src, dst) in enumerate(
            [(q_hbm, qn), (g_hbm, gn), (lt_hbm, ltn), (rd_hbm, rdn), (nb_hbm, nb),
             (pkv_hbm, pkv), (kv_hbm, kv), (proj_hbm, proj)]
        )
    ]
    for load in loads:
        load.start()

    for n, source in ((0, qn), (1, gn)):
        loads[n].wait()
        for i in range(4):
            x = source[32 * i:32 * i + 32, :].astype(F32)
            qg[1, n, 16 * i:16 * i + 16, :] = jnp.concatenate([x[0:8], x[16:24]], 0).astype(BF16)
            qg[1, n, 64 + 16 * i:80 + 16 * i, :] = jnp.concatenate([x[8:16], x[24:32]], 0).astype(BF16)
    for n, source in ((0, ltn), (1, rdn)):
        loads[2 + n].wait()
        x = source[...].reshape(TS, 2, TS, heads)
        x = jnp.concatenate([x[:, 0].reshape(CELLS, heads), x[:, 1].reshape(CELLS, heads)], 0)
        x = jnp.concatenate([x, jnp.zeros((128, 128 - heads), F32)], 1)
        lro[1, 8 * n:8 * n + 8, :] = x.T[0:8]

    pl.semaphore_wait(barrier, 4 + (nw - 1) + (nh - 1) + 1)

    def qg_copy(n):
        dr, dc = STEPS[n]
        return pltpu.make_async_remote_copy(
            src_ref=qg.at[1, :, rows_of(-dc), :],
            dst_ref=qg.at[block_of(dr, dc), :, rows_of(dc), :],
            send_sem=qg_ss.at[n], recv_sem=qg_rs.at[n],
            device_id=at(-dr, -dc), device_id_type=MESH,
        )

    def lr_copy(n):
        dr, dc = STEPS[n]
        return pltpu.make_async_remote_copy(
            src_ref=lro.at[1], dst_ref=lrx.at[n],
            send_sem=lr_ss.at[n], recv_sem=lr_rs.at[n],
            device_id=at(-dr, -dc), device_id_type=MESH,
        )

    def dq_copy(n):
        dr, dc = STEPS[n]
        return pltpu.make_async_remote_copy(
            src_ref=dq_send.at[block_of(dr, dc), rows_of(dc), :],
            dst_ref=dq_recv.at[block_of(-dr, -dc), rows_of(-dc), :],
            send_sem=dq_ss.at[n], recv_sem=dq_rs.at[n],
            device_id=at(dr, dc), device_id_type=MESH,
        )

    for n in range(8):
        lr_copy(n).start()
    for n in range(8):
        qg_copy(n).start()

    loads[5].wait()
    live = lax.broadcasted_iota(jnp.int32, (128, 128), 0) < plen_ref[0]
    for h in range(heads):
        hs = slice(HD * h, HD * h + HD)
        k, v, q, g = pkv[0, :, hs], pkv[1, :, hs], qg[1, 0, :, hs], qg[1, 1, :, hs]
        p = jnp.exp(jnp.where(live, nt(k, q) * factor - lro[1, h:h + 1, :], -BIG))
        ds = (factor * p * (nt(v, g) - lro[1, 8 + h:9 + h, :])).astype(BF16)
        dk = nn(ds, q).reshape(nw, tr, HD)
        dv = nn(p.astype(BF16), g).reshape(nw, tr, HD)
        ps[:, :, hs] = jnp.concatenate([dk, dv], 1).astype(BF16)
        dq_acc[:, hs] = tn(ds, k)

    def p1_copy(peer, slot):
        return pltpu.make_async_remote_copy(
            src_ref=ps.at[peer], dst_ref=pr.at[slot], send_sem=p1_ss.at[peer],
            recv_sem=p1_rs.at[slot], device_id=(ia, peer, it), device_id_type=MESH,
        )

    def p2_copy(peer, slot):
        return pltpu.make_async_remote_copy(
            src_ref=t2.at[peer], dst_ref=r2.at[slot], send_sem=p2_ss.at[peer],
            recv_sem=p2_rs.at[slot], device_id=(peer, iw, it), device_id_type=MESH,
        )

    def p3_copy(peer, slot):
        return pltpu.make_async_remote_copy(
            src_ref=s2, dst_ref=g2.at[slot], send_sem=p3_ss.at[peer],
            recv_sem=p3_rs.at[slot], device_id=(peer, iw, it), device_id_type=MESH,
        )

    def c4_copy(peer, slot):
        return pltpu.make_async_remote_copy(
            src_ref=c4.at[iw], dst_ref=c4.at[slot], send_sem=c4_ss.at[peer],
            recv_sem=c4_rs.at[slot], device_id=(ia, peer, it), device_id_type=MESH,
        )

    def start_all(copy, me, count):
        def body(i, c):
            copy(lax.rem(me + i, count), me).start()
            return c
        lax.fori_loop(1, count, body, 0)

    def wait_all(copy, me, count):
        def body(i, c):
            other = lax.rem(me + i, count)
            copy(other, other).wait_recv()
            return c
        lax.fori_loop(1, count, body, 0)

    def wait_sent(copy, me, count):
        def body(i, c):
            copy(lax.rem(me + i, count), me).wait_send()
            return c
        lax.fori_loop(1, count, body, 0)

    start_all(p1_copy, iw, nw)

    loads[4].wait()
    cols = 2 * nw
    lane = lax.broadcasted_iota(jnp.int32, (1, 128), 1)
    tiles = [(r - 1, c) for r in range(3) for c in (0, 1)] + [(r - 1, c) for r in range(3) for c in (-1, 2)]
    for n, (r, c) in enumerate(tiles):
        row, col = ia + r, 2 * iw + c
        fine = (row >= 0) & (row < nh) & (col >= 0) & (col < cols)
        number = jnp.where(fine, row * cols + col, 0)
        picked[n:n + 1, :] = jnp.where(fine, nb[pl.ds(number, 1), :], -1)
    listed = picked[0:12, :]
    own = ia * cols + 2 * iw
    for side in range(2):
        hit = jnp.max(jnp.where(listed == own + side, 1.0, 0.0), axis=1, keepdims=True)
        hit = jnp.broadcast_to(hit, (12, 128))
        for b in range(6):
            pen[b, side:side + 1, :] = BIG * (1.0 - jnp.where(lane < 64, hit[2 * b:2 * b + 1], hit[2 * b + 1:2 * b + 2]))

    loads[6].wait()

    def attend(b, first=False):
        for h in range(heads):
            hs = slice(HD * h, HD * h + HD)
            k, v, q, g = kv[0, :, hs], kv[1, :, hs], qg[b, 0, :, hs], qg[b, 1, :, hs]
            total = (lro[b, h:h + 1, :] + pen[b, 0:2, :]).reshape(1, 2, 1, 128)
            p = jnp.exp(nt(k, q).reshape(TS, 2, TS, 128) * factor - total).reshape(128, 128)
            ds = (factor * p * (nt(v, g) - lro[b, 8 + h:9 + h, :])).astype(BF16)
            dk, dv = nn(ds, q), nn(p.astype(BF16), g)
            if first:
                dkv_acc[0, :, hs] = dk
                dkv_acc[1, :, hs] = dv
                dq_acc[:, hs] += tn(ds, k)
            else:
                dkv_acc[0, :, hs] += dk
                dkv_acc[1, :, hs] += dv
                dq_send[b, :, hs] = tn(ds, k).astype(BF16)

    def attend_centre(n):
        b = block_of(*STEPS[n])
        lr_copy(n).wait_recv()
        lro[b] = lrx[n]
        qg_copy(n).wait_recv()
        attend(b)
        dq_copy(n).start()

    def attend_outer(west, east):
        b = block_of(*STEPS[west])
        lr_copy(west).wait_recv()
        lr_copy(east).wait_recv()
        both = jnp.where(lax.broadcasted_iota(jnp.int32, (16, 128), 1) < 64, lrx[east], lrx[west])
        lro[b] = pltpu.roll(both, 64, 1)
        qg_copy(west).wait_recv()
        qg_copy(east).wait_recv()
        attend(b)
        dq_copy(west).start()
        dq_copy(east).start()

    attend(1, first=True)
    attend_outer(2, 3)

    wait_all(p1_copy, iw, nw)
    pr[iw] = ps[iw]
    acc = jnp.zeros((2 * tr, width), F32)
    for j in range(nw):
        acc = acc + pr[j].astype(F32)
    t2[...] = jnp.zeros_like(t2)
    for j in range(2 * tr // 8):
        for h in range(heads):
            n = j * heads + h
            t2[n // per_owner, n % per_owner] = acc[8 * j:8 * j + 8, HD * h:HD * h + HD]
    start_all(p2_copy, ia, nh)

    attend_centre(0)
    attend_centre(1)

    wait_all(p2_copy, ia, nh)
    r2[ia] = t2[ia]
    acc = r2[0]
    for j in range(1, nh):
        acc = acc + r2[j]
    s2[...] = acc
    start_all(p3_copy, ia, nh)

    attend_outer(4, 5)

    wait_all(p3_copy, ia, nh)
    g2[ia] = s2[...]
    loads[7].wait()
    groups = []
    for j in range(2 * tr // 8):
        tiles = [g2[(j * heads + h) // per_owner, (j * heads + h) % per_owner] for h in range(heads)]
        groups.append(jnp.concatenate(tiles, 1))
    half = len(groups) // 2
    part = nt(jnp.concatenate(groups[:half], 0).astype(BF16), proj[0])
    part = part + nt(jnp.concatenate(groups[half:], 0).astype(BF16), proj[1])
    c3[0] = part
    c3_copy = pltpu.make_async_remote_copy(
        src_ref=c3.at[0], dst_ref=c3.at[1], send_sem=c3_ss, recv_sem=c3_rs,
        device_id=(ia, iw, 1 - it), device_id_type=MESH,
    )
    c3_copy.start()

    attend_outer(6, 7)
    for n in range(2):
        for i in range(4):
            dkv_out[n, 32 * i:32 * i + 32, :] = dkv_acc[n, 32 * i:32 * i + 32, :].astype(BF16)

    c3_copy.wait_recv()
    c4[iw] = c3[0] + c3[1]
    start_all(c4_copy, iw, nw)

    for n in range(8):
        dq_copy(n).wait_recv()
    for i in range(4):
        left, right = slice(16 * i, 16 * i + 16), slice(64 + 16 * i, 80 + 16 * i)
        sums = []
        for rows in (left, right):
            x = dq_acc[rows, :]
            for b in (0, 2, 3, 4, 5):
                x = x + dq_recv[b, rows, :].astype(F32)
            sums.append(x)
        a, b = sums
        dq_out[32 * i:32 * i + 32, :] = jnp.concatenate([a[0:8], b[0:8], a[8:16], b[8:16]], 0).astype(BF16)

    wait_all(c4_copy, iw, nw)
    for j in range(nw):
        ctx_out[tr * j:tr * j + tr, :] = c4[j]

    for n in range(8):
        qg_copy(n).wait_send()
        lr_copy(n).wait_send()
        dq_copy(n).wait_send()
    c3_copy.wait_send()
    wait_sent(p1_copy, iw, nw)
    wait_sent(p2_copy, ia, nh)
    wait_sent(p3_copy, ia, nh)
    wait_sent(c4_copy, iw, nw)


def solution(mesh):
    nh, nw = mesh.shape["ha"], mesh.shape["wa"]

    def local(queries, keys_values, grad_out, log_totals, row_deltas, prompt_kv, prompt_proj, neighbours, prompt_length):
        rows_here, cols_here, width = queries.shape
        heads = log_totals.shape[-1]
        cells = rows_here * cols_here
        text = prompt_kv.shape[1]
        outs = prompt_proj.shape[1]
        tr = text // nw
        count = 2 * tr // 8 * heads
        per_owner = -(-count // nh)
        any_space = pl.BlockSpec(memory_space=pl.ANY)
        vmem = pl.BlockSpec(memory_space=pltpu.VMEM)
        dma = pltpu.SemaphoreType.DMA
        listed = jnp.pad(neighbours, ((0, 0), (0, 128 - neighbours.shape[1])), constant_values=-1)
        dq, dkv, ctx = pl.pallas_call(
            functools.partial(kernel, nh, nw, heads, per_owner),
            out_shape=(
                jax.ShapeDtypeStruct((cells, width), BF16),
                jax.ShapeDtypeStruct((2, cells, width), BF16),
                jax.ShapeDtypeStruct((text, outs), F32),
            ),
            in_specs=[any_space] * 8 + [pl.BlockSpec(memory_space=pltpu.SMEM)],
            out_specs=(vmem, vmem, vmem),
            scratch_shapes=[
                pltpu.VMEM((cells, width), BF16),
                pltpu.VMEM((2, cells, width), BF16),
                pltpu.VMEM((cells, width), BF16),
                pltpu.VMEM((cells, heads), F32),
                pltpu.VMEM((cells, heads), F32),
                pltpu.VMEM((2, text, width), BF16),
                pltpu.VMEM((2, outs, width), BF16),
                pltpu.VMEM((neighbours.shape[0], 128), jnp.int32),
                pltpu.VMEM((6, 2, cells, width), BF16),
                pltpu.VMEM((8, 16, cells), F32),
                pltpu.VMEM((6, 16, cells), F32),
                pltpu.VMEM((6, 8, cells), F32),
                pltpu.VMEM((16, 128), jnp.int32),
                pltpu.VMEM((cells, width), F32),
                pltpu.VMEM((6, cells, width), BF16),
                pltpu.VMEM((6, cells, width), BF16),
                pltpu.VMEM((2, cells, width), F32),
                pltpu.VMEM((nw, 2 * tr, width), BF16),
                pltpu.VMEM((nw, 2 * tr, width), BF16),
                pltpu.VMEM((nh, per_owner, 8, HD), F32),
                pltpu.VMEM((nh, per_owner, 8, HD), F32),
                pltpu.VMEM((per_owner, 8, HD), F32),
                pltpu.VMEM((nh, per_owner, 8, HD), F32),
                pltpu.VMEM((2, tr, outs), F32),
                pltpu.VMEM((nw, tr, outs), F32),
                dma((8,)),
                dma((8,)), dma((8,)), dma((8,)), dma((8,)), dma((8,)), dma((8,)),
                dma((nw,)), dma((nw,)), dma((nh,)), dma((nh,)), dma((nh,)), dma((nh,)),
                dma, dma, dma((nw,)), dma((nw,)),
            ],
            compiler_params=pltpu.CompilerParams(
                collective_id=0, has_side_effects=True, vmem_limit_bytes=48 * 2**20
            ),
            name="tile_attention_grads",
        )(
            queries.reshape(cells, width), keys_values.reshape(2, cells, width), grad_out.reshape(cells, width),
            log_totals.reshape(cells, heads), row_deltas.reshape(cells, heads),
            prompt_kv, prompt_proj, listed, prompt_length,
        )
        return (
            dq.reshape(rows_here, cols_here, width),
            dkv.reshape(2, rows_here, cols_here, width),
            ctx,
        )

    placed = P("ha", "wa", "ta")
    return jax.shard_map(
        local,
        mesh=mesh,
        in_specs=(placed, P(None, "ha", "wa", "ta"), placed, placed, placed, P(None, None, "ta"), P(None, "ha", "ta"), P(), P()),
        out_specs=(placed, P(None, "ha", "wa", "ta"), P(None, "ha")),
        check_vma=False,
    )
```

time: 1770 us -> 109 us (0.06)
  blocking collectives: 1640 us -> 0 us
  Pallas kernels: 0 us -> 99.2 us
  waiting for transfers between devices: 33.8 us -> 0 us
  starting transfers between devices: 31.4 us -> 0 us
  matrix products: 22 us -> 0 us
    psum x1 -> x0, blocking collectives: 1640 us -> none  [local(): prompt_total = lax.psum(partial_sums, ('ha', 'wa')).astype(jnp.bfloat16)]
    pallas_call x0 -> x1, Pallas kernels: none -> 99.2 us  [local(): pl.pallas_call(functools.partial(kernel, nh, nw, heads, per_owner), out_s...]
    ppermute x8 -> x0, waiting for transfers between devices: 33.8 us -> none  [the longest x4 23.1 us: shifted_2(): return lax.ppermute(x, axis, pairs)]
    ppermute x8 -> x0, starting transfers between devices: 31.4 us -> none  [the longest x4 13.9 us: shifted_2(): return lax.ppermute(x, axis, pairs)]
    dot_general x52 -> x0, matrix products: 22 us -> none  [the longest x10 5.27 us: block_grads(): jnp.einsum('nhmk,nmhe->nkhe', score_grads, queries, preferred_element_typ...]
  transfers between devices with their start and end apart: 9 -> 0, of which waited for: 5 -> 0; matrix products, arithmetic and copies ran while one was open for 2% -> 0% of each run, Pallas kernels for 0% -> 0%
where the time goes in v1:
time: 109 us; the launch traced here: 108 us
  Pallas kernels  99.2 us (91%)
  local copies, waits for them, and re-layouts  7.71 us (7%)
  between operations  1.38 us (1%)
    pallas_call x1, Pallas kernels, local(): pl.pallas_call(functools.partial(kernel, nh, nw, heads, per_owner), out_s...  99.2 us
    unnamed x16, local copies, waits for them, and re-layouts  7.69 us

profile of v1, /device:TPU:8, one launch (start us, length us, event | category | flops | bytes accessed | tf_op | source)
XLA Modules:
  0.0 108.3 jit_solution(11800457634248760483)
XLA Ops:
  0.6 0.0 copy-start
  1.3 0.9 copy.12
  2.2 0.9 copy.13
  3.1 0.0 copy-start.1
  3.1 0.9 copy.14
  4.0 0.0 copy-done
  4.1 0.0 copy-done.1
  4.1 0.0 copy-start.2
  4.1 1.0 copy-done.2
  5.1 0.0 copy-start.3
  5.1 0.9 copy-done.3
  6.0 0.0 copy-start.4
  6.0 0.9 copy-done.4
  6.9 99.2 %tile_attention_grads.1 = (bf16[128,768]{1,0:T(8,128)(2,1)S(1)}, bf16[2,128,768]{2,1,0:T(8,128)(2,1)S(1)}, f32[128,192]{1,0:T(8,128)S(1)}) custom-call(bf16[128,768]{1,0:T(8,128)(2,1)S(1)} %bitcast.11, bf16[2,128,768]{2,1,0:T(8,128)(2,1)S(1)} %bitcast.7, bf16[128,768]{1,0:T(8,128)(2,1)S(1)} %bitcast.12, f32[128,6]{1,0:T(8,128)S(1)} %bitcast.9, ...), custom_call_target="tpu_custom_call" | custom-call | tf_op jit(solution)/shard_map/tile_attention_grads/pallas_call | solution.py:344
  106.2 0.7 copy.15
  106.9 0.7 copy.19
  107.6 0.7 copy.20
  (1 shorter events, 0.0 us)
Async XLA Ops:
  0.6 3.4 %copy-start = (bf16[2,192,768]{2,1,0:T(8,128)(2,1)S(1)}, bf16[2,192,768]{2,1,0:T(8,128)(2,1)}, u32[]{:S(2)}) copy-start(bf16[2,192,768]{2,1,0:T(8,128)(2,1)} %proj_hbm.1) | copy-start | bytes 1769476
  3.1 1.0 copy-start.1
  4.1 1.0 copy-start.2
  5.1 0.9 copy-start.3
  6.0 0.9 copy-start.4

commit v2 on v1

v2 whole, which is shorter than its diff:
```python
import functools

import jax
import jax.numpy as jnp
from jax import lax
from jax.experimental import pallas as pl
from jax.experimental.pallas import tpu as pltpu
from jax.sharding import PartitionSpec as P

MESH = pl.DeviceIdType.MESH
F32 = jnp.float32
BF16 = jnp.bfloat16
TS = 8
CELLS = TS * TS
HD = 128
BIG = 1e30
RING_X = 4
RING_Z = 8
CHUNKS = 2
STEPS = [(-1, 0), (1, 0), (0, -1), (0, 1), (-1, -1), (-1, 1), (1, -1), (1, 1)]
SIDES = (-1, 1)


def block_of(row_step, col_step):
    return row_step + 1 if col_step == 0 else row_step + 4


def rows_of(col_step):
    return {0: slice(0, 128), -1: slice(0, 64), 1: slice(64, 128)}[col_step]


def bit(step):
    return (step + 1) // 2


def nt(a, b):
    return lax.dot_general(a, b, (((1,), (1,)), ((), ())), preferred_element_type=F32)


def nn(a, b):
    return lax.dot_general(a, b, (((1,), (0,)), ((), ())), preferred_element_type=F32)


def tn(a, b):
    return lax.dot_general(a, b, (((0,), (0,)), ((), ())), preferred_element_type=F32)


def kernel(
    nh, nw, heads, per_owner,
    q_hbm, kv_hbm, g_hbm, lt_hbm, rd_hbm, pkv_hbm, proj_hbm, nb_hbm, plen_ref,
    dq_out, dkv_out, ctx_out,
    qn, kv, gn, ltn, rdn, pkv, proj, nb,
    qg, lrx, lro, pen, dqf, dq_send, dq_recv, cx, cz, dkv_acc,
    ps, pa, s1, pb, t2, r2, s2, g2, c3, c4,
    ld_sem, qg_ss, qg_rs, fw_ss, lr_ss, lr_rs, dq_ss, dq_rs, co_ss, cx_rs, cz_rs,
    pa_ss, pa_rs, pb_ss, pb_rs, p2_ss, p2_rs, p3_ss, p3_rs, c3_ss, c3_rs, cy_ss, cy_rs, cw_ss, cw_rs,
):
    width = heads * HD
    nx = min(RING_X, nw)
    ny = nw // nx
    ia, iw, it = lax.axis_index("ha"), lax.axis_index("wa"), lax.axis_index("ta")
    ix, iy = lax.rem(iw, nx), iw // nx
    factor = HD ** -0.5
    tr = 128 // nw
    per_chunk = heads // CHUNKS

    def place(row_step, col_step):
        return lax.rem(ia + row_step + nh, nh), lax.rem(iw + col_step + nw, nw)

    def at(row_step, col_step):
        return place(row_step, col_step) + (it,)

    def seam(column, side):
        return lax.rem(column, RING_X) == (0 if side < 0 else RING_X - 1)

    def by_x(who, row_step, side):
        row, column = who
        across = lax.rem(row, RING_Z) == (0 if row_step < 0 else RING_Z - 1)
        return jnp.logical_or(jnp.logical_not(seam(column, side)), across)

    def lanes(c):
        return slice(HD * per_chunk * c, HD * per_chunk * (c + 1))

    barrier = pltpu.get_barrier_semaphore()

    def greet(who):
        pl.semaphore_signal(barrier, inc=1, device_id=who, device_id_type=MESH)

    def x_peer(i):
        return iy * nx + lax.rem(ix + i, nx)

    def y_peer(i):
        return lax.rem(iy + i, ny) * nx + ix

    def h_peer(i):
        return lax.rem(ia + i, nh)

    def greet_ha(i, c):
        greet((h_peer(i), iw, it))
        return c

    for step in STEPS:
        greet(at(*step))
    for i in range(1, nx):
        greet((ia, x_peer(i), it))
    for i in range(1, ny):
        greet((ia, y_peer(i), it))
    lax.fori_loop(1, nh, greet_ha, 0)
    greet((ia, iw, 1 - it))

    loads = [
        pltpu.make_async_copy(src, dst, ld_sem.at[n])
        for n, (src, dst) in enumerate(
            [(q_hbm, qn), (g_hbm, gn), (lt_hbm, ltn), (rd_hbm, rdn), (nb_hbm, nb),
             (pkv_hbm, pkv), (kv_hbm, kv), (proj_hbm, proj)]
        )
    ]
    for load in loads:
        load.start()

    for n, source in ((0, qn), (1, gn)):
        loads[n].wait()
        for i in range(4):
            x = source[32 * i:32 * i + 32, :].astype(F32)
            qg[1, n, 16 * i:16 * i + 16, :] = jnp.concatenate([x[0:8], x[16:24]], 0).astype(BF16)
            qg[1, n, 64 + 16 * i:80 + 16 * i, :] = jnp.concatenate([x[8:16], x[24:32]], 0).astype(BF16)
    for n, source in ((0, ltn), (1, rdn)):
        loads[2 + n].wait()
        pieces = [source[:, r, TS * s:TS * s + TS] for s in (0, 1) for r in range(TS)]
        lro[1, 8 * n:8 * n + heads, :] = jnp.concatenate(pieces, 1)

    pl.semaphore_wait(barrier, 8 + (nx - 1) + (ny - 1) + (nh - 1) + 1)

    def qg_copy(n, c):
        dr, dc = STEPS[n]
        return pltpu.make_async_remote_copy(
            src_ref=qg.at[1, :, rows_of(-dc), lanes(c)],
            dst_ref=qg.at[block_of(dr, dc), :, rows_of(dc), lanes(c)],
            send_sem=qg_ss.at[c, n % 4], recv_sem=qg_rs.at[c, n],
            device_id=at(-dr, -dc), device_id_type=MESH,
        )

    def forward_x(dr, t, c):
        return pltpu.make_async_remote_copy(
            src_ref=qg.at[block_of(dr, 0), :, rows_of(t), lanes(c)],
            dst_ref=qg.at[block_of(dr, -t), :, rows_of(-t), lanes(c)],
            send_sem=fw_ss.at[c, 2 * bit(dr) + bit(t)], recv_sem=qg_rs.at[c, STEPS.index((dr, -t))],
            device_id=at(0, t), device_id_type=MESH,
        )

    def forward_z(e, s, c):
        return pltpu.make_async_remote_copy(
            src_ref=qg.at[block_of(0, s), :, rows_of(s), lanes(c)],
            dst_ref=qg.at[block_of(-e, s), :, rows_of(s), lanes(c)],
            send_sem=fw_ss.at[c, 4 + 2 * bit(e) + bit(s)], recv_sem=qg_rs.at[c, STEPS.index((-e, s))],
            device_id=at(e, 0), device_id_type=MESH,
        )

    def lr_copy(n):
        dr, dc = STEPS[n]
        return pltpu.make_async_remote_copy(
            src_ref=lro.at[1], dst_ref=lrx.at[n],
            send_sem=lr_ss.at[n], recv_sem=lr_rs.at[n],
            device_id=at(-dr, -dc), device_id_type=MESH,
        )

    def dq_copy(n, c):
        dr, dc = STEPS[n]
        return pltpu.make_async_remote_copy(
            src_ref=dq_send.at[block_of(dr, dc), rows_of(dc), lanes(c)],
            dst_ref=dq_recv.at[block_of(-dr, -dc), rows_of(-dc), lanes(c)],
            send_sem=dq_ss.at[c, n], recv_sem=dq_rs.at[c, n],
            device_id=at(dr, dc), device_id_type=MESH,
        )

    def corner_x(dr, s, c):
        return pltpu.make_async_remote_copy(
            src_ref=dq_send.at[block_of(dr, s), rows_of(s), lanes(c)],
            dst_ref=cx.at[bit(dr), bit(-s), :, lanes(c)],
            send_sem=co_ss.at[c, 2 * bit(dr) + bit(s)], recv_sem=cx_rs.at[c, 2 * bit(dr) + bit(-s)],
            device_id=at(0, s), device_id_type=MESH,
        )

    def corner_z(dr, s, c):
        return pltpu.make_async_remote_copy(
            src_ref=dq_send.at[block_of(dr, s), rows_of(s), lanes(c)],
            dst_ref=cz.at[bit(-dr), bit(s), :, lanes(c)],
            send_sem=co_ss.at[c, 2 * bit(dr) + bit(s)], recv_sem=cz_rs.at[c, 2 * bit(-dr) + bit(s)],
            device_id=at(dr, 0), device_id_type=MESH,
        )

    mine = {(dr, s): by_x((ia, iw), dr, s) for dr in SIDES for s in SIDES}
    relay_x = {(dr, t): by_x(place(0, t), dr, -t) for dr in SIDES for t in SIDES}
    relay_z = {(e, s): jnp.logical_not(by_x(place(e, 0), -e, s)) for e in SIDES for s in SIDES}
    at_seam = {s: seam(iw, s) for s in SIDES}

    for c in range(CHUNKS):
        for n in (2, 3, 0, 1):
            qg_copy(n, c).start()
    for n in range(8):
        lr_copy(n).start()

    loads[5].wait()
    live = lax.broadcasted_iota(jnp.int32, (128, 128), 0) < plen_ref[0]
    for h in range(heads):
        hs = slice(HD * h, HD * h + HD)
        k, v, q, g = pkv[0, :, hs], pkv[1, :, hs], qg[1, 0, :, hs], qg[1, 1, :, hs]
        p = jnp.exp(jnp.where(live, nt(k, q) * factor - lro[1, h:h + 1, :], -BIG))
        ds = (factor * p * (nt(v, g) - lro[1, 8 + h:9 + h, :])).astype(BF16)
        dk = nn(ds, q).reshape(nw, tr, HD)
        dv = nn(p.astype(BF16), g).reshape(nw, tr, HD)
        ps[:, :, hs] = jnp.concatenate([dk, dv], 1).astype(BF16)
        dqf[1, :, hs] = tn(ds, k)

    def pa_copy(i):
        return pltpu.make_async_remote_copy(
            src_ref=ps.at[pl.ds(lax.rem(ix + i, nx) * ny, ny)], dst_ref=pa.at[ix],
            send_sem=pa_ss.at[i], recv_sem=pa_rs.at[i], device_id=(ia, x_peer(i), it), device_id_type=MESH,
        )

    def pb_copy(i):
        return pltpu.make_async_remote_copy(
            src_ref=s1.at[lax.rem(iy + i, ny)], dst_ref=pb.at[iy],
            send_sem=pb_ss.at[i], recv_sem=pb_rs.at[i], device_id=(ia, y_peer(i), it), device_id_type=MESH,
        )

    def p2_copy(peer, slot):
        return pltpu.make_async_remote_copy(
            src_ref=t2.at[peer], dst_ref=r2.at[slot], send_sem=p2_ss.at[peer],
            recv_sem=p2_rs.at[slot], device_id=(peer, iw, it), device_id_type=MESH,
        )

    def p3_copy(peer, slot):
        return pltpu.make_async_remote_copy(
            src_ref=s2, dst_ref=g2.at[slot], send_sem=p3_ss.at[peer],
            recv_sem=p3_rs.at[slot], device_id=(peer, iw, it), device_id_type=MESH,
        )

    def cy_copy(i):
        own_slot = ix * ny + iy
        return pltpu.make_async_remote_copy(
            src_ref=c4.at[own_slot], dst_ref=c4.at[own_slot],
            send_sem=cy_ss.at[i], recv_sem=cy_rs.at[i], device_id=(ia, y_peer(i), it), device_id_type=MESH,
        )

    def cw_copy(i):
        slots = pl.ds(ix * ny, ny)
        return pltpu.make_async_remote_copy(
            src_ref=c4.at[slots], dst_ref=c4.at[slots],
            send_sem=cw_ss.at[i], recv_sem=cw_rs.at[i], device_id=(ia, x_peer(i), it), device_id_type=MESH,
        )

    c3_copy = pltpu.make_async_remote_copy(
        src_ref=c3.at[0], dst_ref=c3.at[1], send_sem=c3_ss, recv_sem=c3_rs,
        device_id=(ia, iw, 1 - it), device_id_type=MESH,
    )

    def start_all(copy):
        def body(i, c):
            copy(h_peer(i), ia).start()
            return c
        lax.fori_loop(1, nh, body, 0)

    def wait_all(copy):
        def body(i, c):
            copy(h_peer(i), h_peer(i)).wait_recv()
            return c
        lax.fori_loop(1, nh, body, 0)

    def wait_sent(copy):
        def body(i, c):
            copy(h_peer(i), ia).wait_send()
            return c
        lax.fori_loop(1, nh, body, 0)

    for i in range(1, nx):
        pa_copy(i).start()

    loads[4].wait()
    cols = 2 * nw
    table = nb.shape[1]
    tiles = [(r - 1, c) for r in range(3) for c in (0, 1)] + [(r - 1, c) for r in range(3) for c in (-1, 2)]
    which = lax.broadcasted_iota(jnp.int32, (16, table), 0)
    numbers = jnp.full((16, table), -5, jnp.int32)
    for n, (r, c) in enumerate(tiles):
        row, col = ia + r, 2 * iw + c
        fine = (row >= 0) & (row < nh) & (col >= 0) & (col < cols)
        numbers = jnp.where(which == n, jnp.where(fine, row * cols + col, -5), numbers)
    chosen = jnp.where(lax.broadcasted_iota(jnp.int32, (16, table), 1) == numbers, 1.0, 0.0)
    lane = lax.broadcasted_iota(jnp.int32, (1, 128), 1)
    for side in range(2):
        hit = jnp.max(jnp.where(nb[...] == ia * cols + 2 * iw + side, 1.0, 0.0), axis=0, keepdims=True)
        hit = jnp.broadcast_to(jnp.max(chosen * hit, axis=1, keepdims=True), (16, 128))
        for b in range(6):
            pen[b, side:side + 1, :] = BIG * (1.0 - jnp.where(lane < 64, hit[2 * b:2 * b + 1], hit[2 * b + 1:2 * b + 2]))

    loads[6].wait()

    def attend(b, c=None, first=False):
        for h in range(heads) if c is None else range(per_chunk * c, per_chunk * (c + 1)):
            hs = slice(HD * h, HD * h + HD)
            k, v, q, g = kv[0, :, hs], kv[1, :, hs], qg[b, 0, :, hs], qg[b, 1, :, hs]
            total = (lro[b, h:h + 1, :] + pen[b, 0:2, :]).reshape(1, 2, 1, 128)
            p = jnp.exp(nt(k, q).reshape(TS, 2, TS, 128) * factor - total).reshape(128, 128)
            ds = (factor * p * (nt(v, g) - lro[b, 8 + h:9 + h, :])).astype(BF16)
            dk, dv = nn(ds, q), nn(p.astype(BF16), g)
            if first:
                dkv_acc[0, :, hs] = dk
                dkv_acc[1, :, hs] = dv
                dqf[b, :, hs] += tn(ds, k)
            else:
                dkv_acc[0, :, hs] += dk
                dkv_acc[1, :, hs] += dv
                dqf[b, :, hs] = tn(ds, k)

    def totals_centre(n):
        lr_copy(n).wait_recv()
        lro[block_of(*STEPS[n])] = lrx[n]

    def totals_outer(west, east):
        lr_copy(west).wait_recv()
        lr_copy(east).wait_recv()
        both = jnp.where(lax.broadcasted_iota(jnp.int32, (16, 128), 1) < 64, lrx[east], lrx[west])
        lro[block_of(*STEPS[west])] = pltpu.roll(both, 64, 1)

    def beside_arrives(c):
        for s in SIDES:
            qg_copy(STEPS.index((0, s)), c).wait_recv()
            for e in SIDES:
                @pl.when(relay_z[e, s])
                def _():
                    forward_z(e, s, c).start()

    def above_below_arrive(c):
        for dr in SIDES:
            qg_copy(STEPS.index((dr, 0)), c).wait_recv()
            for t in SIDES:
                @pl.when(relay_x[dr, t])
                def _():
                    forward_x(dr, t, c).start()

    def send_beside(c, s):
        dq_send[4, rows_of(s), lanes(c)] = dqf[4, rows_of(s), lanes(c)].astype(BF16)
        dq_copy(STEPS.index((0, s)), c).start()

    def attend_beside(c):
        attend(4, c)
        for s in SIDES:
            @pl.when(jnp.logical_not(at_seam[s]))
            def _():
                send_beside(c, s)

    def attend_corners(c):
        for dr in SIDES:
            b = block_of(dr, 1)
            for s in SIDES:
                qg_copy(STEPS.index((dr, s)), c).wait_recv()
            attend(b, c)
            dq_send[b, :, lanes(c)] = dqf[b, :, lanes(c)].astype(BF16)
            for s in SIDES:
                @pl.when(mine[dr, s])
                def _():
                    corner_x(dr, s, c).start()

                @pl.when(jnp.logical_not(mine[dr, s]))
                def _():
                    corner_z(dr, s, c).start()

    def fold(c):
        for s in SIDES:
            for e in SIDES:
                @pl.when(relay_z[e, s])
                def _():
                    corner_z(-e, s, c).wait_recv()
                    dqf[4, rows_of(s), lanes(c)] += cz[bit(e), bit(s), :, lanes(c)].astype(F32)

            @pl.when(at_seam[s])
            def _():
                send_beside(c, s)
        for dr in SIDES:
            for t in SIDES:
                @pl.when(relay_x[dr, t])
                def _():
                    corner_x(dr, -t, c).wait_recv()
                    dqf[dr + 1, rows_of(t), lanes(c)] += cx[bit(dr), bit(t), :, lanes(c)].astype(F32)
            dq_send[dr + 1, :, lanes(c)] = dqf[dr + 1, :, lanes(c)].astype(BF16)
            dq_copy(STEPS.index((dr, 0)), c).start()

    attend(1, first=True)
    totals_outer(2, 3)
    totals_centre(0)
    totals_centre(1)
    for c in range(CHUNKS):
        beside_arrives(c)
        attend_beside(c)
        above_below_arrive(c)
        attend(0, c)
        attend(2, c)
        if c == 0:
            for i in range(1, nx):
                pa_copy(i).wait_recv()
            pa[ix] = ps[pl.ds(ix * ny, ny)]
            for j in range(ny):
                acc = pa[0, j].astype(F32)
                for i in range(1, nx):
                    acc = acc + pa[i, j].astype(F32)
                s1[j] = acc
            for i in range(1, ny):
                pb_copy(i).start()

    for i in range(1, ny):
        pb_copy(i).wait_recv()
    pb[iy] = s1[iy]
    acc = pb[0]
    for j in range(1, ny):
        acc = acc + pb[j]
    t2[...] = jnp.zeros_like(t2)
    for j in range(2 * tr // 8):
        for h in range(heads):
            n = j * heads + h
            t2[n // per_owner, n % per_owner] = acc[8 * j:8 * j + 8, HD * h:HD * h + HD]
    start_all(p2_copy)

    totals_outer(4, 5)
    totals_outer(6, 7)
    attend_corners(0)

    wait_all(p2_copy)
    r2[ia] = t2[ia]
    acc = r2[0]
    for j in range(1, nh):
        acc = acc + r2[j]
    s2[...] = acc
    start_all(p3_copy)

    for c in range(1, CHUNKS):
        attend_corners(c)
    for c in range(CHUNKS):
        fold(c)

    wait_all(p3_copy)
    g2[ia] = s2[...]
    loads[7].wait()
    groups = []
    for j in range(2 * tr // 8):
        tiles = [g2[(j * heads + h) // per_owner, (j * heads + h) % per_owner] for h in range(heads)]
        groups.append(jnp.concatenate(tiles, 1))
    half = len(groups) // 2
    part = nt(jnp.concatenate(groups[:half], 0).astype(BF16), proj[0])
    c3[0] = part + nt(jnp.concatenate(groups[half:], 0).astype(BF16), proj[1])
    c3_copy.start()

    for n in range(2):
        for i in range(4):
            dkv_out[n, 32 * i:32 * i + 32, :] = dkv_acc[n, 32 * i:32 * i + 32, :].astype(BF16)

    c3_copy.wait_recv()
    c4[ix * ny + iy] = c3[0] + c3[1]
    for i in range(1, ny):
        cy_copy(i).start()
    for i in range(1, ny):
        cy_copy(i).wait_recv()
    for i in range(1, nx):
        cw_copy(i).start()

    for c in range(CHUNKS):
        for n in range(4):
            dq_copy(n, c).wait_recv()
    for i in range(4):
        sums = []
        for start in (16 * i, 64 + 16 * i):
            rows = slice(start, start + 16)
            x = dqf[1, rows, :]
            for b in (0, 2, 4):
                x = x + dq_recv[b, rows, :].astype(F32)
            sums.append(x)
        a, b = sums
        dq_out[32 * i:32 * i + 32, :] = jnp.concatenate([a[0:8], b[0:8], a[8:16], b[8:16]], 0).astype(BF16)

    for i in range(1, nx):
        cw_copy(i).wait_recv()
    ctx_out[...] = c4[...].reshape(nw * tr, c4.shape[2]).T

    for c in range(CHUNKS):
        for n in range(4):
            qg_copy(n, c).wait_send()
            dq_copy(n, c).wait_send()
        for a in SIDES:
            for b in SIDES:
                corner_x(a, b, c).wait_send()

                @pl.when(relay_x[a, b])
                def _():
                    forward_x(a, b, c).wait_send()

                @pl.when(relay_z[a, b])
                def _():
                    forward_z(a, b, c).wait_send()
    for n in range(8):
        lr_copy(n).wait_send()
    for i in range(1, nx):
        pa_copy(i).wait_send()
        cw_copy(i).wait_send()
    for i in range(1, ny):
        pb_copy(i).wait_send()
        cy_copy(i).wait_send()
    c3_copy.wait_send()
    wait_sent(p2_copy)
    wait_sent(p3_copy)


def solution(mesh):
    nh, nw = mesh.shape["ha"], mesh.shape["wa"]
    nx = min(RING_X, nw)
    ny = nw // nx

    def local(queries, keys_values, grad_out, log_totals, row_deltas, prompt_kv, prompt_proj, neighbours, prompt_length):
        rows_here, cols_here, width = queries.shape
        heads = log_totals.shape[-1]
        cells = rows_here * cols_here
        text = prompt_kv.shape[1]
        outs = prompt_proj.shape[1]
        tr = text // nw
        count = 2 * tr // 8 * heads
        per_owner = -(-count // nh)
        any_space = pl.BlockSpec(memory_space=pl.ANY)
        vmem = pl.BlockSpec(memory_space=pltpu.VMEM)
        dma = pltpu.SemaphoreType.DMA
        two = lambda n: [dma((n,)), dma((n,))]
        dq, dkv, ctx = pl.pallas_call(
            functools.partial(kernel, nh, nw, heads, per_owner),
            out_shape=(
                jax.ShapeDtypeStruct((cells, width), BF16),
                jax.ShapeDtypeStruct((2, cells, width), BF16),
                jax.ShapeDtypeStruct((outs, text), F32),
            ),
            in_specs=[any_space] * 8 + [pl.BlockSpec(memory_space=pltpu.SMEM)],
            out_specs=(vmem, vmem, vmem),
            scratch_shapes=[
                pltpu.VMEM((cells, width), BF16),
                pltpu.VMEM((2, cells, width), BF16),
                pltpu.VMEM((cells, width), BF16),
                pltpu.VMEM((heads, rows_here, cols_here), F32),
                pltpu.VMEM((heads, rows_here, cols_here), F32),
                pltpu.VMEM((2, text, width), BF16),
                pltpu.VMEM((2, outs, width), BF16),
                pltpu.VMEM(neighbours.shape[::-1], jnp.int32),
                pltpu.VMEM((6, 2, cells, width), BF16),
                pltpu.VMEM((8, 16, cells), F32),
                pltpu.VMEM((6, 16, cells), F32),
                pltpu.VMEM((6, 8, cells), F32),
                pltpu.VMEM((6, cells, width), F32),
                pltpu.VMEM((6, cells, width), BF16),
                pltpu.VMEM((6, cells, width), BF16),
                pltpu.VMEM((2, 2, CELLS, width), BF16),
                pltpu.VMEM((2, 2, CELLS, width), BF16),
                pltpu.VMEM((2, cells, width), F32),
                pltpu.VMEM((nw, 2 * tr, width), BF16),
                pltpu.VMEM((nx, ny, 2 * tr, width), BF16),
                pltpu.VMEM((ny, 2 * tr, width), F32),
                pltpu.VMEM((ny, 2 * tr, width), F32),
                pltpu.VMEM((nh, per_owner, 8, HD), F32),
                pltpu.VMEM((nh, per_owner, 8, HD), F32),
                pltpu.VMEM((per_owner, 8, HD), F32),
                pltpu.VMEM((nh, per_owner, 8, HD), F32),
                pltpu.VMEM((2, tr, outs), F32),
                pltpu.VMEM((nw, tr, outs), F32),
                dma((8,)),
                dma((CHUNKS, 4)), dma((CHUNKS, 8)), dma((CHUNKS, 8)), *two(8),
                dma((CHUNKS, 4)), dma((CHUNKS, 4)), dma((CHUNKS, 4)), dma((CHUNKS, 4)), dma((CHUNKS, 4)),
                *two(nx), *two(ny), *two(nh), *two(nh), dma, dma, *two(ny), *two(nx),
            ],
            compiler_params=pltpu.CompilerParams(
                collective_id=0, has_side_effects=True, vmem_limit_bytes=63 * 2**20
            ),
            name="tile_attention_grads",
        )(
            queries.reshape(cells, width), keys_values.reshape(2, cells, width), grad_out.reshape(cells, width),
            jnp.transpose(log_totals, (2, 0, 1)), jnp.transpose(row_deltas, (2, 0, 1)),
            prompt_kv, prompt_proj, neighbours.T, prompt_length,
        )
        return (
            dq.reshape(rows_here, cols_here, width),
            dkv.reshape(2, rows_here, cols_here, width),
            ctx.T,
        )

    placed = P("ha", "wa", "ta")
    return jax.shard_map(
        local,
        mesh=mesh,
        in_specs=(placed, P(None, "ha", "wa", "ta"), placed, placed, placed, P(None, None, "ta"), P(None, "ha", "ta"), P(), P()),
        out_specs=(placed, P(None, "ha", "wa", "ta"), P(None, "ha")),
        check_vma=False,
    )
```

time: 109 us -> 76.8 us (0.70)
  the two profiles are of different devices: /device:TPU:8 before, /device:TPU:2 now
where the time goes in v2:
time: 76.8 us; the launch traced here: 76.6 us
  Pallas kernels  72 us (94%)
  local copies, waits for them, and re-layouts  3.27 us (4%)
  between operations  1.3 us (2%)
    pallas_call x1, Pallas kernels, local(): pl.pallas_call(functools.partial(kernel, nh, nw, heads, per_owner), out_s...  72 us
    unnamed x7, local copies, waits for them, and re-layouts  3.27 us

profile of v2, /device:TPU:2, one launch (start us, length us, event | category | flops | bytes accessed | tf_op | source)
XLA Modules:
  0.0 76.6 jit_solution(15656501154457505629)
XLA Ops:
  1.3 72.0 %tile_attention_grads.1 = (bf16[128,768]{1,0:T(8,128)(2,1)}, bf16[2,128,768]{2,1,0:T(8,128)(2,1)}, f32[192,128]{1,0:T(8,128)}) custom-call(bf16[128,768]{1,0:T(8,128)(2,1)} %bitcast.12, bf16[2,128,768]{2,1,0:T(8,128)(2,1)} %bitcast.10, bf16[128,768]{1,0:T(8,128)(2,1)} %bitcast.13, f32[6,8,16]{2,1,0:T(8,128)} %bitcast.16, f32[6,8,16]{2,1,0:T(8,128)} %bitcast.17, ...), custom_call_target="tpu_custom_call" | custom-call | tf_op jit(solution)/shard_map/tile_attention_grads/pallas_call | solution.py:530
  73.3 0.0 copy-start
  73.3 1.7 %copy.16 = bf16[8,16,768]{2,1,0:T(8,128)(2,1)} copy(bf16[8,16,768]{2,1,0:T(8,128)(2,1)} %bitcast.11) | data formatting | bytes 393216
  75.0 0.0 copy-done
  75.0 0.0 copy-start.1
  75.0 0.7 copy.17
  75.7 0.2 copy-done.1
  75.9 0.6 copy.18
Async XLA Ops:
  73.3 1.7 %copy-start = (bf16[2,128,768]{2,1,0:T(8,128)(2,1)S(1)}, bf16[2,128,768]{2,1,0:T(8,128)(2,1)}, u32[]{:S(2)}) copy-start(bf16[2,128,768]{2,1,0:T(8,128)(2,1)} %get-tuple-element.7) | copy-start | bytes 1179652
  75.0 1.0 %copy-start.1 = (f32[192,128]{1,0:T(8,128)S(1)}, f32[192,128]{1,0:T(8,128)}, u32[]{:S(2)}) copy-start(f32[192,128]{1,0:T(8,128)} %get-tuple-element.8) | copy-start | bytes 294916

commit v3 on v2

--- a/solution.py
+++ b/solution.py
@@ -46,12 +46,12 @@
 
 
 def kernel(
-    nh, nw, heads, per_owner,
+    nh, nw, heads,
     q_hbm, kv_hbm, g_hbm, lt_hbm, rd_hbm, pkv_hbm, proj_hbm, nb_hbm, plen_ref,
     dq_out, dkv_out, ctx_out,
     qn, kv, gn, ltn, rdn, pkv, proj, nb,
     qg, lrx, lro, pen, dqf, dq_send, dq_recv, cx, cz, dkv_acc,
-    ps, pa, s1, pb, t2, r2, s2, g2, c3, c4,
+    ps, pa, s1, pb, u1, vz, c3, c4,
     ld_sem, qg_ss, qg_rs, fw_ss, lr_ss, lr_rs, dq_ss, dq_rs, co_ss, cx_rs, cz_rs,
     pa_ss, pa_rs, pb_ss, pb_rs, p2_ss, p2_rs, p3_ss, p3_rs, c3_ss, c3_rs, cy_ss, cy_rs, cw_ss, cw_rs,
 ):
@@ -60,6 +60,9 @@
     ny = nw // nx
     ia, iw, it = lax.axis_index("ha"), lax.axis_index("wa"), lax.axis_index("ta")
     ix, iy = lax.rem(iw, nx), iw // nx
+    nz = min(RING_Z, nh)
+    nl = nh // nz
+    iz, il = lax.rem(ia, nz), ia // nz
     factor = HD ** -0.5
     tr = 128 // nw
     per_chunk = heads // CHUNKS
@@ -73,10 +76,23 @@
     def seam(column, side):
         return lax.rem(column, RING_X) == (0 if side < 0 else RING_X - 1)
 
+    def there(row_step):
+        return ia > 0 if row_step < 0 else ia < nh - 1
+
     def by_x(who, row_step, side):
-        row, column = who
-        across = lax.rem(row, RING_Z) == (0 if row_step < 0 else RING_Z - 1)
-        return jnp.logical_or(jnp.logical_not(seam(column, side)), across)
+        return jnp.logical_not(seam(who[1], side))
+
+    def straight(who, row_step, side):
+        if row_step == side:
+            return ia < 0
+        across = lax.rem(who[0], RING_Z) == (0 if row_step < 0 else RING_Z - 1)
+        return jnp.logical_and(seam(who[1], side), across)
+
+    def by_z(who, row_step, side):
+        return jnp.logical_and(seam(who[1], side), jnp.logical_not(straight(who, row_step, side)))
+
+    def both(a, b):
+        return jnp.logical_and(a, b)
 
     def lanes(c):
         return slice(HD * per_chunk * c, HD * per_chunk * (c + 1))
@@ -92,12 +108,11 @@
     def y_peer(i):
         return lax.rem(iy + i, ny) * nx + ix
 
-    def h_peer(i):
-        return lax.rem(ia + i, nh)
-
-    def greet_ha(i, c):
-        greet((h_peer(i), iw, it))
-        return c
+    def l_peer(i):
+        return lax.rem(il + i, nl) * nz + iz
+
+    def z_peer(i):
+        return il * nz + lax.rem(iz + i, nz)
 
     for step in STEPS:
         greet(at(*step))
@@ -105,7 +120,10 @@
         greet((ia, x_peer(i), it))
     for i in range(1, ny):
         greet((ia, y_peer(i), it))
-    lax.fori_loop(1, nh, greet_ha, 0)
+    for i in range(1, nl):
+        greet((l_peer(i), iw, it))
+    for i in range(1, nz):
+        greet((z_peer(i), iw, it))
     greet((ia, iw, 1 - it))
 
     loads = [
@@ -129,14 +147,14 @@
         pieces = [source[:, r, TS * s:TS * s + TS] for s in (0, 1) for r in range(TS)]
         lro[1, 8 * n:8 * n + heads, :] = jnp.concatenate(pieces, 1)
 
-    pl.semaphore_wait(barrier, 8 + (nx - 1) + (ny - 1) + (nh - 1) + 1)
+    pl.semaphore_wait(barrier, 8 + (nx - 1) + (ny - 1) + (nl - 1) + (nz - 1) + 1)
 
     def qg_copy(n, c):
         dr, dc = STEPS[n]
         return pltpu.make_async_remote_copy(
             src_ref=qg.at[1, :, rows_of(-dc), lanes(c)],
             dst_ref=qg.at[block_of(dr, dc), :, rows_of(dc), lanes(c)],
-            send_sem=qg_ss.at[c, n % 4], recv_sem=qg_rs.at[c, n],
+            send_sem=qg_ss.at[c, n], recv_sem=qg_rs.at[c, n],
             device_id=at(-dr, -dc), device_id_type=MESH,
         )
 
@@ -189,17 +207,36 @@
             device_id=at(dr, 0), device_id_type=MESH,
         )
 
-    mine = {(dr, s): by_x((ia, iw), dr, s) for dr in SIDES for s in SIDES}
-    relay_x = {(dr, t): by_x(place(0, t), dr, -t) for dr in SIDES for t in SIDES}
-    relay_z = {(e, s): jnp.logical_not(by_x(place(e, 0), -e, s)) for e in SIDES for s in SIDES}
+    pairs = [(a, b) for a in SIDES for b in SIDES]
+    has = {dr: there(dr) for dr in SIDES}
+    mine_x = {(dr, s): both(has[dr], by_x((ia, iw), dr, s)) for dr, s in pairs}
+    mine_z = {(dr, s): both(has[dr], by_z((ia, iw), dr, s)) for dr, s in pairs}
+    mine_s = {(dr, s): both(has[dr], straight((ia, iw), dr, s)) for dr, s in pairs}
+    relay_x = {(dr, t): both(has[dr], by_x(place(0, t), dr, -t)) for dr, t in pairs}
+    relay_z = {(e, s): both(has[e], by_z(place(e, 0), -e, s)) for e, s in pairs}
+    to_s = {(a, b): both(has[a], straight(place(a, b), -a, -b)) for a, b in pairs}
     at_seam = {s: seam(iw, s) for s in SIDES}
-
-    for c in range(CHUNKS):
-        for n in (2, 3, 0, 1):
-            qg_copy(n, c).start()
+    diagonal = [(a, b) for a, b in pairs if a != b]
+
     for n in range(8):
         lr_copy(n).start()
-
+    for c in range(CHUNKS):
+        for s in SIDES:
+            qg_copy(STEPS.index((0, s)), c).start()
+        for dr in SIDES:
+            @pl.when(has[-dr])
+            def _():
+                qg_copy(STEPS.index((dr, 0)), c).start()
+        for a, b in diagonal:
+            @pl.when(to_s[a, b])
+            def _():
+                qg_copy(STEPS.index((-a, -b)), c).start()
+    for dr in SIDES:
+        @pl.when(jnp.logical_not(has[dr]))
+        def _():
+            qg[dr + 1] = jnp.zeros(qg.shape[1:], BF16)
+            qg[dr + 4] = jnp.zeros(qg.shape[1:], BF16)
+            dq_recv[dr + 1] = jnp.zeros(dq_recv.shape[1:], BF16)
     loads[5].wait()
     live = lax.broadcasted_iota(jnp.int32, (128, 128), 0) < plen_ref[0]
     for h in range(heads):
@@ -224,16 +261,16 @@
             send_sem=pb_ss.at[i], recv_sem=pb_rs.at[i], device_id=(ia, y_peer(i), it), device_id_type=MESH,
         )
 
-    def p2_copy(peer, slot):
-        return pltpu.make_async_remote_copy(
-            src_ref=t2.at[peer], dst_ref=r2.at[slot], send_sem=p2_ss.at[peer],
-            recv_sem=p2_rs.at[slot], device_id=(peer, iw, it), device_id_type=MESH,
-        )
-
-    def p3_copy(peer, slot):
-        return pltpu.make_async_remote_copy(
-            src_ref=s2, dst_ref=g2.at[slot], send_sem=p3_ss.at[peer],
-            recv_sem=p3_rs.at[slot], device_id=(peer, iw, it), device_id_type=MESH,
+    def p2_copy(i):
+        return pltpu.make_async_remote_copy(
+            src_ref=u1.at[il], dst_ref=u1.at[il], send_sem=p2_ss.at[i],
+            recv_sem=p2_rs.at[i], device_id=(l_peer(i), iw, it), device_id_type=MESH,
+        )
+
+    def p3_copy(i):
+        return pltpu.make_async_remote_copy(
+            src_ref=vz.at[iz], dst_ref=vz.at[iz], send_sem=p3_ss.at[i],
+            recv_sem=p3_rs.at[i], device_id=(z_peer(i), iw, it), device_id_type=MESH,
         )
 
     def cy_copy(i):
@@ -254,24 +291,6 @@
         src_ref=c3.at[0], dst_ref=c3.at[1], send_sem=c3_ss, recv_sem=c3_rs,
         device_id=(ia, iw, 1 - it), device_id_type=MESH,
     )
-
-    def start_all(copy):
-        def body(i, c):
-            copy(h_peer(i), ia).start()
-            return c
-        lax.fori_loop(1, nh, body, 0)
-
-    def wait_all(copy):
-        def body(i, c):
-            copy(h_peer(i), h_peer(i)).wait_recv()
-            return c
-        lax.fori_loop(1, nh, body, 0)
-
-    def wait_sent(copy):
-        def body(i, c):
-            copy(h_peer(i), ia).wait_send()
-            return c
-        lax.fori_loop(1, nh, body, 0)
 
     for i in range(1, nx):
         pa_copy(i).start()
@@ -333,7 +352,9 @@
 
     def above_below_arrive(c):
         for dr in SIDES:
-            qg_copy(STEPS.index((dr, 0)), c).wait_recv()
+            @pl.when(has[dr])
+            def _():
+                qg_copy(STEPS.index((dr, 0)), c).wait_recv()
             for t in SIDES:
                 @pl.when(relay_x[dr, t])
                 def _():
@@ -354,17 +375,24 @@
         for dr in SIDES:
             b = block_of(dr, 1)
             for s in SIDES:
-                qg_copy(STEPS.index((dr, s)), c).wait_recv()
+                @pl.when(has[dr])
+                def _():
+                    qg_copy(STEPS.index((dr, s)), c).wait_recv()
             attend(b, c)
             dq_send[b, :, lanes(c)] = dqf[b, :, lanes(c)].astype(BF16)
             for s in SIDES:
-                @pl.when(mine[dr, s])
+                @pl.when(mine_x[dr, s])
                 def _():
                     corner_x(dr, s, c).start()
 
-                @pl.when(jnp.logical_not(mine[dr, s]))
+                @pl.when(mine_z[dr, s])
                 def _():
                     corner_z(dr, s, c).start()
+
+                if (dr, s) in diagonal:
+                    @pl.when(mine_s[dr, s])
+                    def _():
+                        dq_copy(STEPS.index((dr, s)), c).start()
 
     def fold(c):
         for s in SIDES:
@@ -384,118 +412,168 @@
                     corner_x(dr, -t, c).wait_recv()
                     dqf[dr + 1, rows_of(t), lanes(c)] += cx[bit(dr), bit(t), :, lanes(c)].astype(F32)
             dq_send[dr + 1, :, lanes(c)] = dqf[dr + 1, :, lanes(c)].astype(BF16)
-            dq_copy(STEPS.index((dr, 0)), c).start()
+
+            @pl.when(has[dr])
+            def _():
+                dq_copy(STEPS.index((dr, 0)), c).start()
+
+    def sum_over_x():
+        for i in range(1, nx):
+            pa_copy(i).wait_recv()
+        pa[ix] = ps[pl.ds(ix * ny, ny)]
+        for j in range(ny):
+            acc = pa[0, j].astype(F32)
+            for i in range(1, nx):
+                acc = acc + pa[i, j].astype(F32)
+            s1[j] = acc
+        for i in range(1, ny):
+            pb_copy(i).start()
+
+    def sum_over_y():
+        for i in range(1, ny):
+            pb_copy(i).wait_recv()
+        pb[iy] = s1[iy]
+        acc = pb[0]
+        for j in range(1, ny):
+            acc = acc + pb[j]
+        u1[il] = acc
+        for i in range(1, nl):
+            p2_copy(i).start()
+
+    def sum_over_rows():
+        for i in range(1, nl):
+            p2_copy(i).wait_recv()
+        acc = u1[0]
+        for j in range(1, nl):
+            acc = acc + u1[j]
+        vz[iz] = acc.astype(BF16)
+        for i in range(1, nz):
+            p3_copy(i).start()
+
+    def project():
+        for i in range(1, nz):
+            p3_copy(i).wait_recv()
+        loads[7].wait()
+        acc = vz[0].astype(F32)
+        for j in range(1, nz):
+            acc = acc + vz[j].astype(F32)
+        acc = acc.astype(BF16)
+        c3[0] = nt(acc[:tr], proj[0]) + nt(acc[tr:], proj[1])
+        c3_copy.start()
+
+    def gather_over_y():
+        c3_copy.wait_recv()
+        c4[ix * ny + iy] = c3[0] + c3[1]
+        for i in range(1, ny):
+            cy_copy(i).start()
+
+    def gather_over_x():
+        for i in range(1, ny):
+            cy_copy(i).wait_recv()
+        for i in range(1, nx):
+            cw_copy(i).start()
+
+    def write_context():
+        for i in range(1, nx):
+            cw_copy(i).wait_recv()
+        ctx_out[...] = c4[...].reshape(nw * tr, c4.shape[2]).T
+
+    def write_keys():
+        for n in range(2):
+            for i in range(4):
+                dkv_out[n, 32 * i:32 * i + 32, :] = dkv_acc[n, 32 * i:32 * i + 32, :].astype(BF16)
+
+    def write_queries():
+        for c in range(CHUNKS):
+            for s in SIDES:
+                dq_copy(STEPS.index((0, s)), c).wait_recv()
+            for dr in SIDES:
+                @pl.when(has[-dr])
+                def _():
+                    dq_copy(STEPS.index((dr, 0)), c).wait_recv()
+            for a, b in diagonal:
+                @pl.when(to_s[a, b])
+                def _():
+                    dq_copy(STEPS.index((-a, -b)), c).wait_recv()
+                    dqf[1, rows_of(b), lanes(c)] += dq_recv[block_of(a, b), rows_of(b), lanes(c)].astype(F32)
+        for i in range(4):
+            sums = []
+            for start in (16 * i, 64 + 16 * i):
+                rows = slice(start, start + 16)
+                x = dqf[1, rows, :]
+                for b in (0, 2, 4):
+                    x = x + dq_recv[b, rows, :].astype(F32)
+                sums.append(x)
+            a, b = sums
+            dq_out[32 * i:32 * i + 32, :] = jnp.concatenate([a[0:8], b[0:8], a[8:16], b[8:16]], 0).astype(BF16)
 
     attend(1, first=True)
     totals_outer(2, 3)
+    beside_arrives(0)
+    sum_over_x()
+    for c in range(1, CHUNKS):
+        beside_arrives(c)
     totals_centre(0)
     totals_centre(1)
-    for c in range(CHUNKS):
-        beside_arrives(c)
+    above_below_arrive(0)
+    attend_beside(0)
+    sum_over_y()
+    for c in range(1, CHUNKS):
+        above_below_arrive(c)
+    for c in range(1, CHUNKS):
         attend_beside(c)
-        above_below_arrive(c)
+    attend(0, 0)
+    attend(2, 0)
+    sum_over_rows()
+    for c in range(1, CHUNKS):
         attend(0, c)
         attend(2, c)
-        if c == 0:
-            for i in range(1, nx):
-                pa_copy(i).wait_recv()
-            pa[ix] = ps[pl.ds(ix * ny, ny)]
-            for j in range(ny):
-                acc = pa[0, j].astype(F32)
-                for i in range(1, nx):
-                    acc = acc + pa[i, j].astype(F32)
-                s1[j] = acc
-            for i in range(1, ny):
-                pb_copy(i).start()
-
-    for i in range(1, ny):
-        pb_copy(i).wait_recv()
-    pb[iy] = s1[iy]
-    acc = pb[0]
-    for j in range(1, ny):
-        acc = acc + pb[j]
-    t2[...] = jnp.zeros_like(t2)
-    for j in range(2 * tr // 8):
-        for h in range(heads):
-            n = j * heads + h
-            t2[n // per_owner, n % per_owner] = acc[8 * j:8 * j + 8, HD * h:HD * h + HD]
-    start_all(p2_copy)
-
     totals_outer(4, 5)
     totals_outer(6, 7)
     attend_corners(0)
-
-    wait_all(p2_copy)
-    r2[ia] = t2[ia]
-    acc = r2[0]
-    for j in range(1, nh):
-        acc = acc + r2[j]
-    s2[...] = acc
-    start_all(p3_copy)
-
+    project()
     for c in range(1, CHUNKS):
         attend_corners(c)
+    gather_over_y()
     for c in range(CHUNKS):
         fold(c)
-
-    wait_all(p3_copy)
-    g2[ia] = s2[...]
-    loads[7].wait()
-    groups = []
-    for j in range(2 * tr // 8):
-        tiles = [g2[(j * heads + h) // per_owner, (j * heads + h) % per_owner] for h in range(heads)]
-        groups.append(jnp.concatenate(tiles, 1))
-    half = len(groups) // 2
-    part = nt(jnp.concatenate(groups[:half], 0).astype(BF16), proj[0])
-    c3[0] = part + nt(jnp.concatenate(groups[half:], 0).astype(BF16), proj[1])
-    c3_copy.start()
-
-    for n in range(2):
-        for i in range(4):
-            dkv_out[n, 32 * i:32 * i + 32, :] = dkv_acc[n, 32 * i:32 * i + 32, :].astype(BF16)
-
-    c3_copy.wait_recv()
-    c4[ix * ny + iy] = c3[0] + c3[1]
-    for i in range(1, ny):
-        cy_copy(i).start()
-    for i in range(1, ny):
-        cy_copy(i).wait_recv()
-    for i in range(1, nx):
-        cw_copy(i).start()
+    write_keys()
+    gather_over_x()
+    write_queries()
+    write_context()
 
     for c in range(CHUNKS):
-        for n in range(4):
-            dq_copy(n, c).wait_recv()
-    for i in range(4):
-        sums = []
-        for start in (16 * i, 64 + 16 * i):
-            rows = slice(start, start + 16)
-            x = dqf[1, rows, :]
-            for b in (0, 2, 4):
-                x = x + dq_recv[b, rows, :].astype(F32)
-            sums.append(x)
-        a, b = sums
-        dq_out[32 * i:32 * i + 32, :] = jnp.concatenate([a[0:8], b[0:8], a[8:16], b[8:16]], 0).astype(BF16)
-
-    for i in range(1, nx):
-        cw_copy(i).wait_recv()
-    ctx_out[...] = c4[...].reshape(nw * tr, c4.shape[2]).T
-
-    for c in range(CHUNKS):
-        for n in range(4):
-            qg_copy(n, c).wait_send()
-            dq_copy(n, c).wait_send()
-        for a in SIDES:
-            for b in SIDES:
+        for s in SIDES:
+            qg_copy(STEPS.index((0, s)), c).wait_send()
+            dq_copy(STEPS.index((0, s)), c).wait_send()
+
+            @pl.when(has[-s])
+            def _():
+                qg_copy(STEPS.index((s, 0)), c).wait_send()
+
+            @pl.when(has[s])
+            def _():
+                dq_copy(STEPS.index((s, 0)), c).wait_send()
+        for a, b in diagonal:
+            @pl.when(to_s[a, b])
+            def _():
+                qg_copy(STEPS.index((-a, -b)), c).wait_send()
+
+            @pl.when(mine_s[a, b])
+            def _():
+                dq_copy(STEPS.index((a, b)), c).wait_send()
+        for a, b in pairs:
+            @pl.when(both(has[a], jnp.logical_not(mine_s[a, b])))
+            def _():
                 corner_x(a, b, c).wait_send()
 
-                @pl.when(relay_x[a, b])
-                def _():
-                    forward_x(a, b, c).wait_send()
-
-                @pl.when(relay_z[a, b])
-                def _():
-                    forward_z(a, b, c).wait_send()
+            @pl.when(relay_x[a, b])
+            def _():
+                forward_x(a, b, c).wait_send()
+
+            @pl.when(relay_z[a, b])
+            def _():
+                forward_z(a, b, c).wait_send()
     for n in range(8):
         lr_copy(n).wait_send()
     for i in range(1, nx):
@@ -505,14 +583,18 @@
         pb_copy(i).wait_send()
         cy_copy(i).wait_send()
     c3_copy.wait_send()
-    wait_sent(p2_copy)
-    wait_sent(p3_copy)
+    for i in range(1, nl):
+        p2_copy(i).wait_send()
+    for i in range(1, nz):
+        p3_copy(i).wait_send()
 
 
 def solution(mesh):
     nh, nw = mesh.shape["ha"], mesh.shape["wa"]
     nx = min(RING_X, nw)
     ny = nw // nx
+    nz = min(RING_Z, nh)
+    nl = nh // nz
 
     def local(queries, keys_values, grad_out, log_totals, row_deltas, prompt_kv, prompt_proj, neighbours, prompt_length):
         rows_here, cols_here, width = queries.shape
@@ -521,14 +603,12 @@
         text = prompt_kv.shape[1]
         outs = prompt_proj.shape[1]
         tr = text // nw
-        count = 2 * tr // 8 * heads
-        per_owner = -(-count // nh)
         any_space = pl.BlockSpec(memory_space=pl.ANY)
         vmem = pl.BlockSpec(memory_space=pltpu.VMEM)
         dma = pltpu.SemaphoreType.DMA
         two = lambda n: [dma((n,)), dma((n,))]
         dq, dkv, ctx = pl.pallas_call(
-            functools.partial(kernel, nh, nw, heads, per_owner),
+            functools.partial(kernel, nh, nw, heads),
             out_shape=(
                 jax.ShapeDtypeStruct((cells, width), BF16),
                 jax.ShapeDtypeStruct((2, cells, width), BF16),
@@ -559,16 +639,14 @@
                 pltpu.VMEM((nx, ny, 2 * tr, width), BF16),
                 pltpu.VMEM((ny, 2 * tr, width), F32),
                 pltpu.VMEM((ny, 2 * tr, width), F32),
-                pltpu.VMEM((nh, per_owner, 8, HD), F32),
-                pltpu.VMEM((nh, per_owner, 8, HD), F32),
-                pltpu.VMEM((per_owner, 8, HD), F32),
-                pltpu.VMEM((nh, per_owner, 8, HD), F32),
+                pltpu.VMEM((nl, 2 * tr, width), F32),
+                pltpu.VMEM((nz, 2 * tr, width), BF16),
                 pltpu.VMEM((2, tr, outs), F32),
                 pltpu.VMEM((nw, tr, outs), F32),
                 dma((8,)),
-                dma((CHUNKS, 4)), dma((CHUNKS, 8)), dma((CHUNKS, 8)), *two(8),
-                dma((CHUNKS, 4)), dma((CHUNKS, 4)), dma((CHUNKS, 4)), dma((CHUNKS, 4)), dma((CHUNKS, 4)),
-                *two(nx), *two(ny), *two(nh), *two(nh), dma, dma, *two(ny), *two(nx),
+                dma((CHUNKS, 8)), dma((CHUNKS, 8)), dma((CHUNKS, 8)), *two(8),
+                dma((CHUNKS, 8)), dma((CHUNKS, 8)), dma((CHUNKS, 4)), dma((CHUNKS, 4)), dma((CHUNKS, 4)),
+                *two(nx), *two(ny), *two(nl), *two(nz), dma, dma, *two(ny), *two(nx),
             ],
             compiler_params=pltpu.CompilerParams(
                 collective_id=0, has_side_effects=True, vmem_limit_bytes=63 * 2**20

time: 76.8 us -> 67 us (0.87)
  the two profiles are of different devices: /device:TPU:2 before, /device:TPU:14 now
where the time goes in v3:
time: 67 us; the launch traced here: 66.8 us
  Pallas kernels  62.3 us (93%)
  local copies, waits for them, and re-layouts  3.27 us (5%)
  between operations  1.3 us (2%)
    pallas_call x1, Pallas kernels, local(): pl.pallas_call(functools.partial(kernel, nh, nw, heads), out_shape=(jax.S...  62.3 us
    unnamed x7, local copies, waits for them, and re-layouts  3.27 us

profile of v3, /device:TPU:14, one launch (start us, length us, event | category | flops | bytes accessed | tf_op | source)
XLA Modules:
  0.0 66.8 jit_solution(1045729888797347408)
XLA Ops:
  1.3 62.3 %tile_attention_grads.1 = (bf16[128,768]{1,0:T(8,128)(2,1)}, bf16[2,128,768]{2,1,0:T(8,128)(2,1)}, f32[192,128]{1,0:T(8,128)}) custom-call(bf16[128,768]{1,0:T(8,128)(2,1)} %bitcast.12, bf16[2,128,768]{2,1,0:T(8,128)(2,1)} %bitcast.10, bf16[128,768]{1,0:T(8,128)(2,1)} %bitcast.13, f32[6,8,16]{2,1,0:T(8,128)} %bitcast.16, f32[6,8,16]{2,1,0:T(8,128)} %bitcast.17, ...), custom_call_target="tpu_custom_call" | custom-call | tf_op jit(solution)/shard_map/tile_attention_grads/pallas_call | solution.py:610
  63.6 0.0 copy-start
  63.6 1.7 %copy.16 = bf16[8,16,768]{2,1,0:T(8,128)(2,1)} copy(bf16[8,16,768]{2,1,0:T(8,128)(2,1)} %bitcast.11) | data formatting | bytes 393216
  65.2 0.0 copy-done
  65.2 0.0 copy-start.1
  65.2 0.7 %copy.17 = bf16[2,8,16,768]{3,2,1,0:T(8,128)(2,1)} copy(bf16[2,8,16,768]{3,2,1,0:T(8,128)(2,1)S(1)} %bitcast.9) | data formatting | bytes 786432
  66.0 0.2 copy-done.1
  66.2 0.6 copy.18
Async XLA Ops:
  63.6 1.7 %copy-start = (bf16[2,128,768]{2,1,0:T(8,128)(2,1)S(1)}, bf16[2,128,768]{2,1,0:T(8,128)(2,1)}, u32[]{:S(2)}) copy-start(bf16[2,128,768]{2,1,0:T(8,128)(2,1)} %get-tuple-element.7) | copy-start | bytes 1179652
  65.2 1.0 %copy-start.1 = (f32[192,128]{1,0:T(8,128)S(1)}, f32[192,128]{1,0:T(8,128)}, u32[]{:S(2)}) copy-start(f32[192,128]{1,0:T(8,128)} %get-tuple-element.8) | copy-start | bytes 294916

commit v4 on v3

--- a/solution.py
+++ b/solution.py
@@ -50,9 +50,9 @@
     q_hbm, kv_hbm, g_hbm, lt_hbm, rd_hbm, pkv_hbm, proj_hbm, nb_hbm, plen_ref,
     dq_out, dkv_out, ctx_out,
     qn, kv, gn, ltn, rdn, pkv, proj, nb,
-    qg, lrx, lro, pen, dqf, dq_send, dq_recv, cx, cz, dkv_acc,
+    qg, held, lrx, lro, pen, dqf, dq_send, dq_recv, cx, cz, dkv_acc,
     ps, pa, s1, pb, u1, vz, c3, c4,
-    ld_sem, qg_ss, qg_rs, fw_ss, lr_ss, lr_rs, dq_ss, dq_rs, co_ss, cx_rs, cz_rs,
+    ld_sem, qg_ss, qg_rs, fw_ss, hp_ss, hp_rs, hf_ss, lr_ss, lr_rs, dq_ss, dq_rs, co_ss, cx_rs, cz_rs,
     pa_ss, pa_rs, pb_ss, pb_rs, p2_ss, p2_rs, p3_ss, p3_rs, c3_ss, c3_rs, cy_ss, cy_rs, cw_ss, cw_rs,
 ):
     width = heads * HD
@@ -174,6 +174,20 @@
             device_id=at(e, 0), device_id_type=MESH,
         )
 
+    def hop_copy(dr):
+        return pltpu.make_async_remote_copy(
+            src_ref=qg.at[1, :, :, lanes(CHUNKS - 1)], dst_ref=held.at[bit(dr)],
+            send_sem=hp_ss.at[bit(dr)], recv_sem=hp_rs.at[bit(dr)],
+            device_id=(il * nz + lax.rem(iz - dr + nz, nz), iw, it), device_id_type=MESH,
+        )
+
+    def hop_forward(dr):
+        return pltpu.make_async_remote_copy(
+            src_ref=held.at[bit(dr)], dst_ref=qg.at[block_of(dr, 0), :, :, lanes(CHUNKS - 1)],
+            send_sem=hf_ss.at[bit(dr)], recv_sem=qg_rs.at[CHUNKS - 1, STEPS.index((dr, 0))],
+            device_id=(lax.rem(ia - dr * nz + nh, nh), iw, it), device_id_type=MESH,
+        )
+
     def lr_copy(n):
         dr, dc = STEPS[n]
         return pltpu.make_async_remote_copy(
@@ -216,6 +230,16 @@
     relay_z = {(e, s): both(has[e], by_z(place(e, 0), -e, s)) for e, s in pairs}
     to_s = {(a, b): both(has[a], straight(place(a, b), -a, -b)) for a, b in pairs}
     at_seam = {s: seam(iw, s) for s in SIDES}
+    crowded = {-1: ix == nx - 1, 1: ix == 0}
+    hops = {
+        -1: both(crowded[-1], both(iz == nz - 1, has[1])),
+        1: both(crowded[1], both(iz == 0, has[-1])),
+    }
+    relays = {
+        -1: both(crowded[-1], both(iz == 0, ia + nz < nh)),
+        1: both(crowded[1], both(iz == nz - 1, ia >= nz)),
+    }
+    passes = {dr: both(has[-dr], jnp.logical_not(hops[dr])) for dr in SIDES}
     diagonal = [(a, b) for a, b in pairs if a != b]
 
     for n in range(8):
@@ -224,9 +248,14 @@
         for s in SIDES:
             qg_copy(STEPS.index((0, s)), c).start()
         for dr in SIDES:
-            @pl.when(has[-dr])
+            @pl.when(passes[dr] if c == CHUNKS - 1 else has[-dr])
             def _():
                 qg_copy(STEPS.index((dr, 0)), c).start()
+
+            if c == CHUNKS - 1:
+                @pl.when(hops[dr])
+                def _():
+                    hop_copy(dr).start()
         for a, b in diagonal:
             @pl.when(to_s[a, b])
             def _():
@@ -508,6 +537,11 @@
             dq_out[32 * i:32 * i + 32, :] = jnp.concatenate([a[0:8], b[0:8], a[8:16], b[8:16]], 0).astype(BF16)
 
     attend(1, first=True)
+    for dr in SIDES:
+        @pl.when(relays[dr])
+        def _():
+            hop_copy(dr).wait_recv()
+            hop_forward(dr).start()
     totals_outer(2, 3)
     beside_arrives(0)
     sum_over_x()
@@ -547,7 +581,7 @@
             qg_copy(STEPS.index((0, s)), c).wait_send()
             dq_copy(STEPS.index((0, s)), c).wait_send()
 
-            @pl.when(has[-s])
+            @pl.when(passes[s] if c == CHUNKS - 1 else has[-s])
             def _():
                 qg_copy(STEPS.index((s, 0)), c).wait_send()
 
@@ -574,6 +608,14 @@
             @pl.when(relay_z[a, b])
             def _():
                 forward_z(a, b, c).wait_send()
+    for dr in SIDES:
+        @pl.when(hops[dr])
+        def _():
+            hop_copy(dr).wait_send()
+
+        @pl.when(relays[dr])
+        def _():
+            hop_forward(dr).wait_send()
     for n in range(8):
         lr_copy(n).wait_send()
     for i in range(1, nx):
@@ -626,6 +668,7 @@
                 pltpu.VMEM((2, outs, width), BF16),
                 pltpu.VMEM(neighbours.shape[::-1], jnp.int32),
                 pltpu.VMEM((6, 2, cells, width), BF16),
+                pltpu.VMEM((2, 2, cells, width // CHUNKS), BF16),
                 pltpu.VMEM((8, 16, cells), F32),
                 pltpu.VMEM((6, 16, cells), F32),
                 pltpu.VMEM((6, 8, cells), F32),
@@ -644,7 +687,7 @@
                 pltpu.VMEM((2, tr, outs), F32),
                 pltpu.VMEM((nw, tr, outs), F32),
                 dma((8,)),
-                dma((CHUNKS, 8)), dma((CHUNKS, 8)), dma((CHUNKS, 8)), *two(8),
+                dma((CHUNKS, 8)), dma((CHUNKS, 8)), dma((CHUNKS, 8)), dma((2,)), *two(2), *two(8),
                 dma((CHUNKS, 8)), dma((CHUNKS, 8)), dma((CHUNKS, 4)), dma((CHUNKS, 4)), dma((CHUNKS, 4)),
                 *two(nx), *two(ny), *two(nl), *two(nz), dma, dma, *two(ny), *two(nx),
             ],

time: 67 us -> 64.3 us (0.960)
  the two profiles are of different devices: /device:TPU:14 before, /device:TPU:8 now
where the time goes in v4:
time: 64.3 us; the launch traced here: 64.1 us
  Pallas kernels  59.6 us (93%)
  local copies, waits for them, and re-layouts  3.27 us (5%)
  between operations  1.3 us (2%)
    pallas_call x1, Pallas kernels, local(): pl.pallas_call(functools.partial(kernel, nh, nw, heads), out_shape=(jax.S...  59.6 us
    unnamed x7, local copies, waits for them, and re-layouts  3.27 us

profile of v4, /device:TPU:8, one launch (start us, length us, event | category | flops | bytes accessed | tf_op | source)
XLA Modules:
  0.0 64.1 jit_solution(3018659126787309567)
XLA Ops:
  1.3 59.6 %tile_attention_grads.1 = (bf16[128,768]{1,0:T(8,128)(2,1)}, bf16[2,128,768]{2,1,0:T(8,128)(2,1)}, f32[192,128]{1,0:T(8,128)}) custom-call(bf16[128,768]{1,0:T(8,128)(2,1)} %bitcast.12, bf16[2,128,768]{2,1,0:T(8,128)(2,1)} %bitcast.10, bf16[128,768]{1,0:T(8,128)(2,1)} %bitcast.13, f32[6,8,16]{2,1,0:T(8,128)} %bitcast.16, f32[6,8,16]{2,1,0:T(8,128)} %bitcast.17, ...), custom_call_target="tpu_custom_call" | custom-call | tf_op jit(solution)/shard_map/tile_attention_grads/pallas_call | solution.py:652
  60.9 0.0 copy-start
  60.9 1.7 %copy.16 = bf16[8,16,768]{2,1,0:T(8,128)(2,1)} copy(bf16[8,16,768]{2,1,0:T(8,128)(2,1)} %bitcast.11) | data formatting | bytes 393216
  62.5 0.0 copy-done
  62.5 0.0 copy-start.1
  62.5 0.7 %copy.17 = bf16[2,8,16,768]{3,2,1,0:T(8,128)(2,1)} copy(bf16[2,8,16,768]{3,2,1,0:T(8,128)(2,1)S(1)} %bitcast.9) | data formatting | bytes 786432
  63.3 0.2 copy-done.1
  63.5 0.6 copy.18
Async XLA Ops:
  60.9 1.7 %copy-start = (bf16[2,128,768]{2,1,0:T(8,128)(2,1)S(1)}, bf16[2,128,768]{2,1,0:T(8,128)(2,1)}, u32[]{:S(2)}) copy-start(bf16[2,128,768]{2,1,0:T(8,128)(2,1)} %get-tuple-element.7) | copy-start | bytes 1179652
  62.5 1.0 %copy-start.1 = (f32[192,128]{1,0:T(8,128)S(1)}, f32[192,128]{1,0:T(8,128)}, u32[]{:S(2)}) copy-start(f32[192,128]{1,0:T(8,128)} %get-tuple-element.8) | copy-start | bytes 294916

commit v5 on v4

--- a/solution.py
+++ b/solution.py
@@ -569,9 +569,9 @@
     for c in range(1, CHUNKS):
         attend_corners(c)
     gather_over_y()
+    write_keys()
     for c in range(CHUNKS):
         fold(c)
-    write_keys()
     gather_over_x()
     write_queries()
     write_context()
@@ -629,6 +629,19 @@
         p2_copy(i).wait_send()
     for i in range(1, nz):
         p3_copy(i).wait_send()
+
+
+def deliver(a_in, b_in, c_in, a_out, b_out, c_out, a_mid, b_mid, c_mid, in_sem, out_sem):
+    parts = [(b_in, b_mid, b_out), (a_in, a_mid, a_out), (c_in, c_mid, c_out)]
+    reads = [pltpu.make_async_copy(src, mid, in_sem.at[n]) for n, (src, mid, _) in enumerate(parts)]
+    writes = [pltpu.make_async_copy(mid, dst, out_sem.at[n]) for n, (_, mid, dst) in enumerate(parts)]
+    for read in reads:
+        read.start()
+    for read, write in zip(reads, writes):
+        read.wait()
+        write.start()
+    for write in writes:
+        write.wait()
 
 
 def solution(mesh):
@@ -700,6 +713,16 @@
             jnp.transpose(log_totals, (2, 0, 1)), jnp.transpose(row_deltas, (2, 0, 1)),
             prompt_kv, prompt_proj, neighbours.T, prompt_length,
         )
+        results = (dq, dkv, ctx)
+        dq, dkv, ctx = pl.pallas_call(
+            deliver,
+            out_shape=tuple(jax.ShapeDtypeStruct(x.shape, x.dtype) for x in results),
+            in_specs=[any_space] * 3,
+            out_specs=(any_space,) * 3,
+            scratch_shapes=[pltpu.VMEM(x.shape, x.dtype) for x in results] + two(3),
+            compiler_params=pltpu.CompilerParams(vmem_limit_bytes=62 * 2**20),
+            name="deliver",
+        )(*results)
         return (
             dq.reshape(rows_here, cols_here, width),
             dkv.reshape(2, rows_here, cols_here, width),

time: 64.3 us -> 62.9 us (0.978)
  local copies, waits for them, and re-layouts: 3.27 us -> 0 us
  Pallas kernels: 59.6 us -> 61.4 us
    unnamed x7 -> x0, local copies, waits for them, and re-layouts: 3.27 us -> none
    pallas_call x0 -> x1, Pallas kernels: none -> 1.88 us  [local(): pl.pallas_call(deliver, out_shape=tuple((jax.ShapeDtypeStruct(x.shape, x....]
where the time goes in v5:
time: 62.9 us; the launch traced here: 62.7 us
  Pallas kernels  61.4 us (98%)
  between operations  1.29 us (2%)
    pallas_call x1, Pallas kernels, local(): pl.pallas_call(functools.partial(kernel, nh, nw, heads), out_shape=(jax.S...  59.6 us
    pallas_call x1, Pallas kernels, local(): pl.pallas_call(deliver, out_shape=tuple((jax.ShapeDtypeStruct(x.shape, x....  1.88 us

profile of v5, /device:TPU:8, one launch (start us, length us, event | category | flops | bytes accessed | tf_op | source)
XLA Modules:
  0.0 62.7 jit_solution(15775629664275886241)
XLA Ops:
  1.3 59.6 %tile_attention_grads.1 = (bf16[128,768]{1,0:T(8,128)(2,1)}, bf16[2,128,768]{2,1,0:T(8,128)(2,1)}, f32[192,128]{1,0:T(8,128)}) custom-call(bf16[128,768]{1,0:T(8,128)(2,1)} %bitcast.10, bf16[2,128,768]{2,1,0:T(8,128)(2,1)} %bitcast.9, bf16[128,768]{1,0:T(8,128)(2,1)} %bitcast.11, f32[6,8,16]{2,1,0:T(8,128)} %bitcast.13, f32[6,8,16]{2,1,0:T(8,128)} %bitcast.14, ...), custom_call_target="tpu_custom_call" | custom-call | tf_op jit(solution)/shard_map/tile_attention_grads/pallas_call | solution.py:665
  60.9 1.9 %deliver.1 = (bf16[128,768]{1,0:T(8,128)(2,1)}, bf16[2,128,768]{2,1,0:T(8,128)(2,1)}, f32[192,128]{1,0:T(8,128)}) custom-call(bf16[128,768]{1,0:T(8,128)(2,1)} %get-tuple-element.9.a_in, bf16[2,128,768]{2,1,0:T(8,128)(2,1)} %get-tuple-element.10.b_in, f32[192,128]{1,0:T(8,128)} %get-tuple-element.11.c_in), custom_call_target="tpu_custom_call" | custom-call | tf_op jit(solution)/shard_map/deliver/pallas_call | solution.py:717

commit v6 on v5

--- a/solution.py
+++ b/solution.py
@@ -49,7 +49,7 @@
     nh, nw, heads,
     q_hbm, kv_hbm, g_hbm, lt_hbm, rd_hbm, pkv_hbm, proj_hbm, nb_hbm, plen_ref,
     dq_out, dkv_out, ctx_out,
-    qn, kv, gn, ltn, rdn, pkv, proj, nb,
+    keys_low, key_sem, qn, kv, gn, ltn, rdn, pkv, proj, nb,
     qg, held, lrx, lro, pen, dqf, dq_send, dq_recv, cx, cz, dkv_acc,
     ps, pa, s1, pb, u1, vz, c3, c4,
     ld_sem, qg_ss, qg_rs, fw_ss, hp_ss, hp_rs, hf_ss, lr_ss, lr_rs, dq_ss, dq_rs, co_ss, cx_rs, cz_rs,
@@ -510,7 +510,7 @@
     def write_keys():
         for n in range(2):
             for i in range(4):
-                dkv_out[n, 32 * i:32 * i + 32, :] = dkv_acc[n, 32 * i:32 * i + 32, :].astype(BF16)
+                keys_low[n, 32 * i:32 * i + 32, :] = dkv_acc[n, 32 * i:32 * i + 32, :].astype(BF16)
 
     def write_queries():
         for c in range(CHUNKS):
@@ -570,11 +570,14 @@
         attend_corners(c)
     gather_over_y()
     write_keys()
+    key_move = pltpu.make_async_copy(keys_low, dkv_out, key_sem)
+    key_move.start()
     for c in range(CHUNKS):
         fold(c)
     gather_over_x()
     write_queries()
     write_context()
+    key_move.wait()
 
     for c in range(CHUNKS):
         for s in SIDES:
@@ -670,8 +673,10 @@
                 jax.ShapeDtypeStruct((outs, text), F32),
             ),
             in_specs=[any_space] * 8 + [pl.BlockSpec(memory_space=pltpu.SMEM)],
-            out_specs=(vmem, vmem, vmem),
+            out_specs=(vmem, any_space, vmem),
             scratch_shapes=[
+                pltpu.VMEM((2, cells, width), BF16),
+                dma,
                 pltpu.VMEM((cells, width), BF16),
                 pltpu.VMEM((2, cells, width), BF16),
                 pltpu.VMEM((cells, width), BF16),

time: 62.9 us -> 62.8 us (level)
  no operation moved by 1% of the time
where the time goes in v6:
time: 62.8 us; the launch traced here: 62.6 us
  Pallas kernels  61.3 us (98%)
  between operations  1.29 us (2%)
    pallas_call x1, Pallas kernels, local(): pl.pallas_call(functools.partial(kernel, nh, nw, heads), out_shape=(jax.S...  59.4 us
    pallas_call x1, Pallas kernels, local(): pl.pallas_call(deliver, out_shape=tuple((jax.ShapeDtypeStruct(x.shape, x....  1.88 us

profile of v6, /device:TPU:8, one launch (start us, length us, event | category | flops | bytes accessed | tf_op | source)
XLA Modules:
  0.0 62.6 jit_solution(1055526407737156701)
XLA Ops:
  1.3 59.4 %tile_attention_grads.1 = (bf16[128,768]{1,0:T(8,128)(2,1)}, bf16[2,128,768]{2,1,0:T(8,128)(2,1)}, f32[192,128]{1,0:T(8,128)}) custom-call(bf16[128,768]{1,0:T(8,128)(2,1)} %bitcast.10, bf16[2,128,768]{2,1,0:T(8,128)(2,1)} %bitcast.9, bf16[128,768]{1,0:T(8,128)(2,1)} %bitcast.11, f32[6,8,16]{2,1,0:T(8,128)} %bitcast.13, f32[6,8,16]{2,1,0:T(8,128)} %bitcast.14, ...), custom_call_target="tpu_custom_call" | custom-call | tf_op jit(solution)/shard_map/tile_attention_grads/pallas_call | solution.py:668
  60.7 1.9 %deliver.1 = (bf16[128,768]{1,0:T(8,128)(2,1)}, bf16[2,128,768]{2,1,0:T(8,128)(2,1)}, f32[192,128]{1,0:T(8,128)}) custom-call(bf16[128,768]{1,0:T(8,128)(2,1)} %get-tuple-element.9.a_in, bf16[2,128,768]{2,1,0:T(8,128)(2,1)} %get-tuple-element.10.b_in, f32[192,128]{1,0:T(8,128)} %get-tuple-element.11.c_in), custom_call_target="tpu_custom_call" | custom-call | tf_op jit(solution)/shard_map/deliver/pallas_call | solution.py:722
